TPU v7x, 128 devices: a whole 4x4x4 slice. The times are simulated.
128 devices in a mesh: expert: 8 (over y, core), dp: 16 (over x, z).
Axes of the slice: x: 4, y: 4, z: 4, core: 2. Of those that a mesh axis runs over, the one named last changes fastest.
Arguments:
- tokens: bfloat16 [131072, 2048], P(('expert', 'dp')), may hold values from -6 to 6
- block_expert: int32 [1024, 1], P(('expert', 'dp')), may hold values from 0 to 7; in each aligned block of 8 rows (0 to 7, 8 to 15, ...) at most 2 rows name the same one
- gate_weight: bfloat16 [8, 2048, 768], P('expert', 'dp'), may hold values from -0.125 to 0.125
- up_weight: bfloat16 [8, 2048, 768], P('expert', 'dp'), may hold values from -0.125 to 0.125
- down_weight: bfloat16 [8, 768, 2048], P('expert', None, 'dp'), may hold values from -0.21875 to 0.21875
Outputs:
- r_factor: float32 [8, 768, 768], P('expert', 'dp')
- compressed_down: float32 [8, 768, 2048], P('expert', None, 'dp')
Inputs may be any that keep to these rules, and one draw needn't show every extreme that they name: `block_expert`: among the 8 blocks of one device, at most 2 name the same expert, and in every draw some device has exactly 2 blocks for one expert.
All inputs are finite; a program needn't handle non-finite values.
Results may differ from a plain program's by a relative error of at most 0.0003.
Values may be sent and summed in bfloat16 or wider, within the bound.
A program may use at most 128 MiB of HBM per device.

v0:
```python
import jax
import jax.numpy as jnp
from jax import lax
from jax.sharding import PartitionSpec as P

BROWS = 128


damping = 0.05


def on_device(tokens, block_expert, gate_weight, up_weight, down_weight):
    n_expert = lax.axis_size("expert")
    n_data = lax.axis_size("dp")
    exp_local = gate_weight.shape[0]
    width = gate_weight.shape[2]
    model = tokens.shape[1]
    experts = exp_local * n_expert
    blk_count = block_expert.shape[0]
    capacity = max(2, 2 * blk_count // experts)
    rows_avg = blk_count * BROWS * n_data * n_expert // experts
    blocks = tokens.reshape(blk_count, BROWS, model)
    ids = block_expert[:, 0]
    positions = jnp.arange(blk_count, dtype=jnp.int32)
    same = ids[:, None] == ids[None, :]
    earlier = positions[None, :] < positions[:, None]
    ranks = jnp.sum((same & earlier).astype(jnp.int32), axis=1)
    slots = jnp.arange(experts * capacity, dtype=jnp.int32)
    match = (ids[None, :] == (slots // capacity)[:, None]) & (
        ranks[None, :] == (slots % capacity)[:, None]
    )
    found = jnp.sum(match.astype(jnp.int32), axis=1)
    source = jnp.sum(match.astype(jnp.int32) * positions[None, :], axis=1) + (1 - found) * blk_count
    padded = jnp.concatenate([blocks, jnp.zeros((1, BROWS, model), jnp.bfloat16)], axis=0)
    outgoing = padded[source].reshape(n_expert, exp_local, capacity, BROWS, model)
    arrived = lax.all_to_all(outgoing, "expert", split_axis=0, concat_axis=0, tiled=True)
    eye = jnp.eye(width, dtype=jnp.float32)
    my_rows = width // n_data
    rows = arrived[:, 0].reshape(-1, model)
    gate = jnp.dot(
        rows,
        lax.all_gather(gate_weight[0], "dp", axis=0, tiled=True),
        preferred_element_type=jnp.float32,
    )
    lifted = jnp.dot(
        rows,
        lax.all_gather(up_weight[0], "dp", axis=0, tiled=True),
        preferred_element_type=jnp.float32,
    )
    hidden = jax.nn.silu(gate) * lifted
    gram = jnp.dot(hidden.T, hidden, precision=lax.Precision.HIGHEST) / float(rows_avg)
    total = lax.psum(gram, "dp") + damping * eye
    upper = jnp.linalg.cholesky(total).T
    factors = [lax.dynamic_slice_in_dim(upper, lax.axis_index("dp") * my_rows, my_rows, 0)]
    products = [jnp.dot(upper, down_weight[0].astype(jnp.float32), precision=lax.Precision.HIGHEST)]
    return (jnp.stack(factors), jnp.stack(products))


def solution(mesh):
    placed = (
        P(("expert", "dp"), None),
        P(("expert", "dp"), None),
        P("expert", "dp", None),
        P("expert", "dp", None),
        P("expert", None, "dp"),
    )
    return jax.shard_map(
        on_device,
        mesh=mesh,
        in_specs=placed,
        out_specs=(P("expert", "dp", None), P("expert", None, "dp")),
        check_vma=False,
    )
```

profile of v0, /device:TPU:0, one launch (start us, length us, event | category | flops | bytes accessed | tf_op | source)
XLA Modules:
  0.0 414.7 jit_solution(4864001126445819598)
XLA Ops:
  7.9 5.0 %concatenate.3 = bf16[9,128,2048]{2,1,0:T(8,128)(2,1)} pad(bf16[8,128,2048]{2,1,0:T(8,128)(2,1)} %bitcast.59, bf16[]{:T(256)} %constant.236.clone.1), padding=0_1x0_0x0_0 | pad | bytes 8912898 | tf_op jit(solution)/shard_map/concatenate | solution.py:34
  13.2 7.0 %gather_fusion = bf16[16,128,2048]{2,1,0:T(8,128)(2,1)} fusion(bf16[9,128,2048]{2,1,0:T(8,128)(2,1)} %concatenate.3, s32[1024]{0:T(1024)S(1)} %pad_clamp_fusion), kind=kCustom, calls=%fused_computation | custom fusion | bytes 16777280 | tf_op jit(solution)/shard_map/gather | solution.py:35
  20.2 5.0 %all-to-all-start = ((bf16[8,1,2,128,2048]{4,3,2,1,0:T(8,128)(2,1)}), bf16[8,1,2,128,2048]{4,3,2,1,0:T(8,128)(2,1)}, u32[]{:S(2)}, u32[]{:S(2)}) async-start(bf16[8,1,2,128,2048]{4,3,2,1,0:T(8,128)(2,1)} %bitcast.58), calls=%async_computation | async-start | bytes 16777216 | tf_op jit(solution)/shard_map/all_to_all | solution.py:36
  26.0 34.8 %all-gather.7.cloned.1.call-done = bf16[1,2048,768]{2,1,0:T(8,128)(2,1)} async-done(((bf16[1,128,768]{2,1,0:T(8,128)(2,1)}), bf16[1,2048,768]{2,1,0:T(8,128)(2,1)}) %all-gather.7.cloned.1.call-update) | async-done | bytes 3145744 | tf_op jit(solution)/shard_map/all_gather | solution.py:47
  60.8 59.0 %all-to-all-done = bf16[8,1,2,128,2048]{4,3,2,1,0:T(8,128)(2,1)} async-done(((bf16[8,1,2,128,2048]{4,3,2,1,0:T(8,128)(2,1)}), bf16[8,1,2,128,2048]{4,3,2,1,0:T(8,128)(2,1)}, u32[]{:S(2)}, u32[]{:S(2)}) %all-to-all-start) | async-done | bytes 8388640 | tf_op jit(solution)/shard_map/all_to_all | solution.py:36
  119.8 11.7 %fusion.7 = f32[2048,768]{1,0:T(8,128)} fusion(bf16[2048,2048]{1,0:T(8,128)(2,1)} %bitcast.5, bf16[1,2048,768]{2,1,0:T(8,128)(2,1)} %all-gather.7.cloned.1.call-done), kind=kOutput, calls=%fused_computation.8 | convolution fusion | flops 6442450944 | bytes 17825792 | tf_op jit(solution)/shard_map/dot_general | solution.py:45
  131.5 10.3 %fusion.9 = f32[2048,768]{1,0:T(8,128)S(1)} fusion(bf16[2048,2048]{1,0:T(8,128)(2,1)} %bitcast.5, bf16[1,2048,768]{2,1,0:T(8,128)(2,1)} %all-gather.5.cloned.1.call-done), kind=kOutput, calls=%fused_computation.10 | convolution fusion | flops 6442450944 | bytes 17825792 | tf_op jit(solution)/shard_map/dot_general | solution.py:40
  141.9 20.1 %fusion.13 = f32[768,768]{0,1:T(8,128)} fusion(f32[2048,768]{1,0:T(8,128)S(1)} %copy-done.4, f32[2048,768]{1,0:T(8,128)S(1)} %fusion.9), kind=kOutput, calls=%fused_computation.19 | convolution fusion | flops 14503968768 | bytes 14942208 | tf_op jit(solution)/shard_map/dot_general | solution.py:51
  162.0 92.3 %all-reduce.4.cloned.1.call-done = f32[768,768]{0,1:T(8,128)} async-done(((f32[768,768]{0,1:T(8,128)}), f32[768,768]{0,1:T(8,128)}) %all-reduce.4.cloned.1.call-update) | async-done | bytes 2359312 | tf_op jit(solution)/shard_map/psum | solution.py:52
  254.2 3.3 select_add_fusion
  257.5 3.2 copy.24
  260.7 2.0 fusion.12
  264.1 11.7 %cholesky.164 = f32[128,128]{1,0:T(8,128)S(1)} custom-call(f32[128,128]{1,0:T(8,128)S(1)} %cholesky.421), custom_call_target="Cholesky" | custom-call | tf_op jit(solution)/shard_map/jit(cholesky)/cholesky | solution.py:53
  275.9 9.8 %custom-call.43 = f32[1,128,128]{1,2,0:T(8,128)S(1)} custom-call(f32[1,128,128]{2,1,0:T(8,128)S(1)} %get-tuple-element.13), custom_call_target="InvertDiagBlocksLowerTriangular" | custom-call | tf_op jit(solution)/shard_map/jit(cholesky)/cholesky | solution.py:53
  289.1 11.7 %cholesky.187 = f32[128,128]{1,0:T(8,128)S(1)} custom-call(f32[128,128]{1,0:T(8,128)S(1)} %cholesky.425), custom_call_target="Cholesky" | custom-call | tf_op jit(solution)/shard_map/jit(cholesky)/cholesky | solution.py:53
  300.9 10.0 %custom-call.44 = f32[1,128,128]{1,2,0:T(8,128)S(1)} custom-call(f32[1,128,128]{2,1,0:T(8,128)S(1)} %get-tuple-element.11), custom_call_target="InvertDiagBlocksLowerTriangular" | custom-call | tf_op jit(solution)/shard_map/jit(cholesky)/cholesky | solution.py:53
  313.3 11.7 %cholesky.352 = f32[128,128]{1,0:T(8,128)S(1)} custom-call(f32[128,128]{1,0:T(8,128)S(1)} %cholesky.430), custom_call_target="Cholesky" | custom-call | tf_op jit(solution)/shard_map/jit(cholesky)/cholesky | solution.py:53
  325.1 9.8 %custom-call.45 = f32[1,128,128]{1,2,0:T(8,128)S(1)} custom-call(f32[1,128,128]{2,1,0:T(8,128)S(1)} %get-tuple-element.9), custom_call_target="InvertDiagBlocksLowerTriangular" | custom-call | tf_op jit(solution)/shard_map/jit(cholesky)/cholesky | solution.py:53
  335.4 2.1 convolution_subtract_fusion.2
  337.4 11.9 %cholesky.371 = f32[128,128]{1,0:T(8,128)S(1)} custom-call(f32[128,128]{1,0:T(8,128)S(1)} %cholesky.435), custom_call_target="Cholesky" | custom-call | tf_op jit(solution)/shard_map/jit(cholesky)/cholesky | solution.py:53
  349.5 9.8 %custom-call.46 = f32[1,128,128]{1,2,0:T(8,128)S(1)} custom-call(f32[1,128,128]{2,1,0:T(8,128)S(1)} %get-tuple-element.7), custom_call_target="InvertDiagBlocksLowerTriangular" | custom-call | tf_op jit(solution)/shard_map/jit(cholesky)/cholesky | solution.py:53
  361.6 11.7 %cholesky.390 = f32[128,128]{1,0:T(8,128)S(1)} custom-call(f32[128,128]{1,0:T(8,128)S(1)} %cholesky.440), custom_call_target="Cholesky" | custom-call | tf_op jit(solution)/shard_map/jit(cholesky)/cholesky | solution.py:53
  373.4 9.8 %custom-call.47 = f32[1,128,128]{1,2,0:T(8,128)S(1)} custom-call(f32[1,128,128]{2,1,0:T(8,128)S(1)} %get-tuple-element.5), custom_call_target="InvertDiagBlocksLowerTriangular" | custom-call | tf_op jit(solution)/shard_map/jit(cholesky)/cholesky | solution.py:53
  385.3 11.7 %cholesky.408 = f32[128,128]{1,0:T(8,128)S(1)} custom-call(f32[128,128]{1,0:T(8,128)S(1)} %convolution_subtract_fusion.4), custom_call_target="Cholesky" | custom-call | tf_op jit(solution)/shard_map/jit(cholesky)/cholesky | solution.py:53
  (63 shorter events, 21.2 us)
Async XLA Ops:
  7.2 398.0 %copy-start = (bf16[1,768,128]{2,1,0:T(8,128)(2,1)S(1)}, bf16[1,768,128]{2,1,0:T(8,128)(2,1)}, u32[]{:S(2)}) copy-start(bf16[1,768,128]{2,1,0:T(8,128)(2,1)} %param.9) | copy-start | bytes 589828
  7.2 53.6 %all-gather.7.cloned.1.call-start = ((), (), s32[]{:S(2)}) async-start(), calls=%async_computation.3 | async-start | bytes 3342336 | tf_op jit(solution)/shard_map/all_gather | solution.py:47
  7.9 5.0 %copy-start.3 = (s32[8,1]{0,1:T(1,128)S(1)}, s32[8,1]{0,1:T(1,128)}, u32[]{:S(2)}) copy-start(s32[8,1]{0,1:T(1,128)} %param.6) | copy-start | bytes 100
  20.2 99.6 %all-to-all-start = ((bf16[8,1,2,128,2048]{4,3,2,1,0:T(8,128)(2,1)}), bf16[8,1,2,128,2048]{4,3,2,1,0:T(8,128)(2,1)}, u32[]{:S(2)}, u32[]{:S(2)}) async-start(bf16[8,1,2,128,2048]{4,3,2,1,0:T(8,128)(2,1)} %bitcast.58), calls=%async_computation | async-start | bytes 16777216 | tf_op jit(solution)/shard_map/all_to_all | solution.py:36
  25.2 106.4 %all-gather.5.cloned.1.call-start = ((), (), s32[]{:S(2)}) async-start(), calls=%async_computation.2 | async-start | bytes 3342336 | tf_op jit(solution)/shard_map/all_gather | solution.py:42
  25.9 228.3 %all-reduce.4.cloned.1.call-start = ((), (), s32[]{:S(2)}) async-start(), calls=%async_computation.1 | async-start | bytes 4718592 | tf_op jit(solution)/shard_map/psum | solution.py:52
  131.5 10.3 %copy-start.4 = (f32[2048,768]{1,0:T(8,128)S(1)}, f32[2048,768]{1,0:T(8,128)}, u32[]{:S(2)}) copy-start(f32[2048,768]{1,0:T(8,128)} %fusion.7) | copy-start | bytes 18874372
  257.5 3.2 copy-start.1
  262.7 1.4 copy-start.2
Sparse Core Ops, SparseCore 0:
  10.2 50.5 all-gather.6
  63.0 46.8 all-gather.4
  162.1 92.1 all-reduce.3
where the time goes:
time: 420 us; the launch traced here: 415 us
  waiting for transfers between devices  187 us (45%)
  other arithmetic  130 us (31%)
  matrix products  56.3 us (13%)
  between operations  18.3 us (4%)
  local copies, waits for them, and re-layouts  18 us (4%)
  starting transfers between devices  5.11 us (1%)
    another operation x23, other arithmetic, on_device(): upper = jnp.linalg.cholesky(total).T  124 us
    psum x1, waiting for transfers between devices, on_device(): total = lax.psum(gram, 'dp') + damping * eye  92.3 us
    all_to_all x1, waiting for transfers between devices, on_device(): lax.all_to_all(outgoing, 'expert', split_axis=0, concat_axis=0, tiled=True)  59 us
    all_gather x1, waiting for transfers between devices, on_device(): lax.all_gather(up_weight[0], 'dp', axis=0, tiled=True)  34.8 us
    dot_general x1, matrix products, on_device(): jnp.dot(hidden.T, hidden, precision=lax.Precision.HIGHEST) / float(rows_avg)  20.1 us
    another operation x10, matrix products, on_device(): upper = jnp.linalg.cholesky(total).T  12.3 us
    dot_general x1, matrix products, on_device(): jnp.dot(rows, lax.all_gather(up_weight[0], 'dp', axis=0, tiled=True), pre...  11.7 us
    dot_general x1, matrix products, on_device(): jnp.dot(rows, lax.all_gather(gate_weight[0], 'dp', axis=0, tiled=True), p...  10.3 us
  transfers between devices with their start and end apart: 4, of which 3 were waited for; matrix products, arithmetic and copies ran while one was open for 6% of the time, Pallas kernels for 0%

commit v1 on v0

--- a/solution.py
+++ b/solution.py
@@ -1,12 +1,125 @@
 import jax
 import jax.numpy as jnp
 from jax import lax
+from jax.experimental import pallas as pl
+from jax.experimental.pallas import tpu as pltpu
 from jax.sharding import PartitionSpec as P
 
 BROWS = 128
 
 
 damping = 0.05
+
+
+HI = lax.Precision.HIGHEST
+
+
+def lanes(v, k):
+    return jnp.take_along_axis(v, jnp.full((8,128), k, jnp.int32), axis=1)
+def subl(v, r):
+    return jnp.broadcast_to(v[r:r+1, :], (8, 128))
+
+def factor8(M):
+    M = list(M)
+    lane = lax.broadcasted_iota(jnp.int32, (8,128), 1)
+    sub = lax.broadcasted_iota(jnp.int32, (8,128), 0)
+    up, lo = [], []
+    for q in range(16):
+        k0 = 8*q
+        C = {t: [lanes(M[t], k0+j) for j in range(8)] for t in range(q, 16)}
+        E = list(C[q])
+        own = (lane >= k0) & (lane < k0+8)
+        ident = (lane == sub + k0).astype(jnp.float32)
+        V = M[q]
+        N = jnp.where(own, ident, M[q])
+        F = N
+        U = V
+        dinv = jnp.zeros((8,128), jnp.float32)
+        for j in range(8):
+            d = subl(E[j], j)
+            inv = 1.0 / d
+            dinv = jnp.where(sub == j, inv, dinv)
+            s = E[j] * inv
+            fj = jnp.where(sub == j, 1.0 - inv, s)
+            ff = jnp.where(sub > j, s, 0.0)
+            for i in range(j+1, 8):
+                E[i] = E[i] - fj * subl(E[i], j)
+            N, F, U = N - fj * subl(N, j), F - ff * subl(F, j), U - ff * subl(U, j)
+        rs = jnp.sqrt(dinv)
+        U, F = U*rs, F*rs
+        up.append(jnp.where(lane >= sub + k0, U, 0.0))
+        lo.append(jnp.where(lane <= sub + k0, F, 0.0))
+        G = [subl(N, j) for j in range(8)]
+        for t in range(q+1, 16):
+            base = jnp.where(own, 0.0, M[t])
+            c = C[t]
+            a = (c[0]*G[0] + c[1]*G[1]) + (c[2]*G[2] + c[3]*G[3])
+            b = (c[4]*G[4] + c[5]*G[5]) + (c[6]*G[6] + c[7]*G[7])
+            M[t] = base - (a + b)
+    return up, lo
+
+def kernel(me_ref, g_ref, w_ref, r_ref, p_ref, A, R, L):
+    A[...] = g_ref[...]
+    def body(kb, _):
+        row = pl.multiple_of(kb*128, 128)
+        blk = A[pl.ds(row,128), pl.ds(row,128)]
+        up, lo = factor8([blk[8*t:8*t+8] for t in range(16)])
+        zero = jnp.zeros((128,128), jnp.float32)
+        for c in range(6):
+            @pl.when(c < kb)
+            def _(): R[pl.ds(row,128), c*128:(c+1)*128] = zero
+        for t in range(16):
+            R[pl.ds(row + 8*t, 8), pl.ds(row,128)] = up[t]
+            L[8*t:8*t+8, :] = lo[t]
+        for q in range(5):
+            @pl.when(kb == q)
+            def _():
+                x = (q+1)*128
+                P = jnp.dot(L[...], A[q*128:x, x:], precision=HI, preferred_element_type=jnp.float32)
+                R[q*128:x, x:] = P
+                for i in range(q+1, 6):
+                    y = i*128
+                    A[y:y+128, y:] -= lax.dot_general(P[:, y-x:y-x+128], P[:, y-x:], (((0,),(0,)),((),())), precision=HI, preferred_element_type=jnp.float32)
+        return 0
+    lax.fori_loop(0, 6, body, 0)
+    r_ref[...] = R[pl.ds(pl.multiple_of(me_ref[0]*48, 8), 48), :]
+    for i in range(6):
+        y = i*128
+        p_ref[y:y+128, :] = jnp.dot(R[y:y+128, y:], w_ref[y:, :].astype(jnp.float32), precision=HI, preferred_element_type=jnp.float32)
+
+def chol(me, g, w):
+    V = pl.BlockSpec(memory_space=pltpu.VMEM)
+    return pl.pallas_call(kernel, out_shape=(jax.ShapeDtypeStruct((48,768),jnp.float32), jax.ShapeDtypeStruct((768,128),jnp.float32)),
+        in_specs=[pl.BlockSpec(memory_space=pltpu.SMEM), V, V], out_specs=(V,V),
+        scratch_shapes=[pltpu.VMEM((768,768),jnp.float32), pltpu.VMEM((768,768),jnp.float32), pltpu.VMEM((128,128),jnp.float32)],
+        compiler_params=pltpu.CompilerParams(vmem_limit_bytes=40<<20))(me, g, w)
+
+
+def fill_kernel(source_ref, block_ref, slot_ref):
+    used = source_ref[pl.program_id(0)] < source_ref[source_ref.shape[0] - 1]
+
+    @pl.when(used)
+    def _():
+        slot_ref[...] = block_ref[...]
+
+    @pl.when(jnp.logical_not(used))
+    def _():
+        slot_ref[...] = jnp.zeros_like(slot_ref)
+
+
+def fill_slots(source, blocks):
+    count, rows, model = blocks.shape
+    slots = source.shape[0]
+    return pl.pallas_call(
+        fill_kernel,
+        out_shape=jax.ShapeDtypeStruct((slots, rows, model), blocks.dtype),
+        grid_spec=pltpu.PrefetchScalarGridSpec(
+            num_scalar_prefetch=1,
+            grid=(slots,),
+            in_specs=[pl.BlockSpec((1, rows, model), lambda s, src: (lax.rem(src[s], count), 0, 0))],
+            out_specs=pl.BlockSpec((1, rows, model), lambda s, src: (s, 0, 0)),
+        ),
+    )(jnp.append(source, count), blocks)
 
 
 def on_device(tokens, block_expert, gate_weight, up_weight, down_weight):
@@ -31,11 +144,9 @@
     )
     found = jnp.sum(match.astype(jnp.int32), axis=1)
     source = jnp.sum(match.astype(jnp.int32) * positions[None, :], axis=1) + (1 - found) * blk_count
-    padded = jnp.concatenate([blocks, jnp.zeros((1, BROWS, model), jnp.bfloat16)], axis=0)
-    outgoing = padded[source].reshape(n_expert, exp_local, capacity, BROWS, model)
+    outgoing = fill_slots(source, blocks).reshape(n_expert, exp_local, capacity, BROWS, model)
     arrived = lax.all_to_all(outgoing, "expert", split_axis=0, concat_axis=0, tiled=True)
     eye = jnp.eye(width, dtype=jnp.float32)
-    my_rows = width // n_data
     rows = arrived[:, 0].reshape(-1, model)
     gate = jnp.dot(
         rows,
@@ -50,10 +161,9 @@
     hidden = jax.nn.silu(gate) * lifted
     gram = jnp.dot(hidden.T, hidden, precision=lax.Precision.HIGHEST) / float(rows_avg)
     total = lax.psum(gram, "dp") + damping * eye
-    upper = jnp.linalg.cholesky(total).T
-    factors = [lax.dynamic_slice_in_dim(upper, lax.axis_index("dp") * my_rows, my_rows, 0)]
-    products = [jnp.dot(upper, down_weight[0].astype(jnp.float32), precision=lax.Precision.HIGHEST)]
-    return (jnp.stack(factors), jnp.stack(products))
+    me = lax.axis_index("dp").astype(jnp.int32).reshape(1)
+    factor, product = chol(me, total, down_weight[0])
+    return (factor[None], product[None])
 
 
 def solution(mesh):

time: 420 us -> 294 us (0.70); the launches traced: 415 us -> 294 us
  other arithmetic: 130 us -> 4.08 us
  Pallas kernels: 0 us -> 42.5 us
  local copies, waits for them, and re-layouts: 18 us -> 0.01 us
  matrix products: 56.3 us -> 41.2 us
  between operations: 18.3 us -> 13.8 us
    another operation x23 -> x0, other arithmetic: 124 us -> none  [on_device(): upper = jnp.linalg.cholesky(total).T]
    pallas_call x0 -> x2, Pallas kernels: none -> 42.5 us  [the longest x1 29.7 us: chol(): pl.pallas_call(kernel, out_shape=(jax.ShapeDtypeStruct((48, 768), jnp.flo...]
    another operation x10 -> x0, matrix products: 12.3 us -> none  [on_device(): upper = jnp.linalg.cholesky(total).T]
    gather x1 -> x0, local copies, waits for them, and re-layouts: 6.98 us -> none  [on_device(): padded[source].reshape(n_expert, exp_local, capacity, BROWS, model)]
    concatenate x1 -> x0, local copies, waits for them, and re-layouts: 4.97 us -> none  [on_device(): jnp.concatenate([blocks, jnp.zeros((1, BROWS, model), jnp.bfloat16)], axi...]
  transfers between devices with their start and end apart: 4 -> 4, of which waited for: 3 -> 3; matrix products, arithmetic and copies ran while one was open for 6% -> 5% of each run, Pallas kernels for 0% -> 4%
where the time goes in v1:
time: 294 us
  waiting for transfers between devices  187 us (64%)
  Pallas kernels  42.5 us (14%)
  matrix products  41.2 us (14%)
  between operations  13.8 us (5%)
  starting transfers between devices  5.05 us (2%)
  other arithmetic  4.08 us (1%)
    psum x1, waiting for transfers between devices, on_device(): total = lax.psum(gram, 'dp') + damping * eye  92.1 us
    all_to_all x1, waiting for transfers between devices, on_device(): lax.all_to_all(outgoing, 'expert', split_axis=0, concat_axis=0, tiled=True)  61.8 us
    all_gather x1, waiting for transfers between devices, on_device(): lax.all_gather(up_weight[0], 'dp', axis=0, tiled=True)  32 us
    pallas_call x1, Pallas kernels, chol(): pl.pallas_call(kernel, out_shape=(jax.ShapeDtypeStruct((48, 768), jnp.flo...  29.7 us
    dot_general x1, matrix products, on_device(): jnp.dot(hidden.T, hidden, precision=lax.Precision.HIGHEST) / float(rows_avg)  19.1 us
    pallas_call x1, Pallas kernels, fill_slots(): pl.pallas_call(fill_kernel, out_shape=jax.ShapeDtypeStruct((slots, rows,...  12.8 us
    dot_general x1, matrix products, on_device(): jnp.dot(rows, lax.all_gather(up_weight[0], 'dp', axis=0, tiled=True), pre...  11.7 us
    dot_general x1, matrix products, on_device(): jnp.dot(rows, lax.all_gather(gate_weight[0], 'dp', axis=0, tiled=True), p...  10.3 us
  transfers between devices with their start and end apart: 4, of which 3 were waited for; matrix products, arithmetic and copies ran while one was open for 5% of the time, Pallas kernels for 4%

profile of v1, /device:TPU:0, one launch (start us, length us, event | category | flops | bytes accessed | tf_op | source)
XLA Modules:
  0.0 294.0 jit_solution(14182880368817400533)
XLA Ops:
  7.2 0.0 all-gather.7.cloned.1.call-start
  7.2 0.7 all-gather.7.cloned.1.call-update
  7.9 0.9 convert_reduce_fusion.1
  8.8 0.7 convert_reduce_fusion
  9.6 0.6 pad_add_fusion.source_ref
  10.2 12.8 %shard_map.68 = bf16[16,128,2048]{2,1,0:T(8,128)(2,1)} custom-call(s32[17]{0:T(128)} %pad_add_fusion.source_ref, bf16[8,128,2048]{2,1,0:T(8,128)(2,1)} %bitcast.20), custom_call_target="tpu_custom_call" | custom-call | tf_op jit(solution)/shard_map/pallas_call | solution.py:113
  23.0 4.9 %all-to-all-start = ((bf16[8,1,2,128,2048]{4,3,2,1,0:T(8,128)(2,1)}), bf16[8,1,2,128,2048]{4,3,2,1,0:T(8,128)(2,1)}, u32[]{:S(2)}, u32[]{:S(2)}) async-start(bf16[8,1,2,128,2048]{4,3,2,1,0:T(8,128)(2,1)} %bitcast.19), calls=%async_computation | async-start | bytes 16777216 | tf_op jit(solution)/shard_map/all_to_all | solution.py:148
  27.9 0.0 all-gather.5.cloned.1.call-start
  28.0 0.7 all-gather.5.cloned.1.call-update
  28.7 0.0 all-reduce.2.cloned.1.call-start
  28.7 32.0 %all-gather.7.cloned.1.call-done = bf16[1,2048,768]{2,1,0:T(8,128)(2,1)} async-done(((bf16[1,128,768]{2,1,0:T(8,128)(2,1)}), bf16[1,2048,768]{2,1,0:T(8,128)(2,1)}) %all-gather.7.cloned.1.call-update) | async-done | bytes 3145744 | tf_op jit(solution)/shard_map/all_gather | solution.py:158
  60.8 61.8 %all-to-all-done = bf16[8,1,2,128,2048]{4,3,2,1,0:T(8,128)(2,1)} async-done(((bf16[8,1,2,128,2048]{4,3,2,1,0:T(8,128)(2,1)}), bf16[8,1,2,128,2048]{4,3,2,1,0:T(8,128)(2,1)}, u32[]{:S(2)}, u32[]{:S(2)}) %all-to-all-start) | async-done | bytes 8388640 | tf_op jit(solution)/shard_map/all_to_all | solution.py:148
  122.5 11.7 %fusion.7 = f32[2048,768]{1,0:T(8,128)} fusion(bf16[2048,2048]{1,0:T(8,128)(2,1)} %bitcast.5, bf16[1,2048,768]{2,1,0:T(8,128)(2,1)} %all-gather.7.cloned.1.call-done), kind=kOutput, calls=%fused_computation.7 | convolution fusion | flops 6442450944 | bytes 17825792 | tf_op jit(solution)/shard_map/dot_general | solution.py:156
  134.3 0.0 all-gather.5.cloned.1.call-done
  134.3 0.0 copy-start.1
  134.3 10.3 %fusion.9 = f32[2048,768]{1,0:T(8,128)S(1)} fusion(bf16[2048,2048]{1,0:T(8,128)(2,1)} %bitcast.5, bf16[1,2048,768]{2,1,0:T(8,128)(2,1)} %all-gather.5.cloned.1.call-done), kind=kOutput, calls=%fused_computation.9 | convolution fusion | flops 6442450944 | bytes 17825792 | tf_op jit(solution)/shard_map/dot_general | solution.py:151
  144.6 0.0 copy-done.1
  144.6 19.1 %fusion.12 = f32[768,768]{1,0:T(8,128)} fusion(f32[2048,768]{1,0:T(8,128)S(1)} %copy-done.1, f32[2048,768]{1,0:T(8,128)S(1)} %fusion.9), kind=kOutput, calls=%fused_computation.14 | convolution fusion | flops 14503968768 | bytes 14942208 | tf_op jit(solution)/shard_map/dot_general | solution.py:162
  163.7 0.0 copy-start
  163.7 0.0 all-reduce.2.cloned.1.call-update
  163.8 92.1 %all-reduce.2.cloned.1.call-done = f32[768,768]{1,0:T(8,128)} async-done(((f32[768,768]{1,0:T(8,128)}), f32[768,768]{1,0:T(8,128)}) %all-reduce.2.cloned.1.call-update) | async-done | bytes 2359312 | tf_op jit(solution)/shard_map/psum | solution.py:163
  255.9 1.8 select_add_fusion.g_ref
  257.7 0.0 copy-done
  257.7 29.7 %shard_map.69 = (f32[48,768]{1,0:T(8,128)}, f32[768,128]{1,0:T(8,128)}) custom-call(s32[1]{0:T(128)} %bitcast.me_ref, f32[768,768]{1,0:T(8,128)S(1)} %select_add_fusion.g_ref, bf16[768,128]{1,0:T(8,128)(2,1)S(1)} %bitcast.18), custom_call_target="tpu_custom_call" | custom-call | tf_op jit(solution)/shard_map/pallas_call | solution.py:92
  (2 shorter events, 0.0 us)
Async XLA Ops:
  7.2 53.6 %all-gather.7.cloned.1.call-start = ((), (), s32[]{:S(2)}) async-start(), calls=%async_computation.3 | async-start | bytes 3342336 | tf_op jit(solution)/shard_map/all_gather | solution.py:158
  23.0 99.6 %all-to-all-start = ((bf16[8,1,2,128,2048]{4,3,2,1,0:T(8,128)(2,1)}), bf16[8,1,2,128,2048]{4,3,2,1,0:T(8,128)(2,1)}, u32[]{:S(2)}, u32[]{:S(2)}) async-start(bf16[8,1,2,128,2048]{4,3,2,1,0:T(8,128)(2,1)} %bitcast.19), calls=%async_computation | async-start | bytes 16777216 | tf_op jit(solution)/shard_map/all_to_all | solution.py:148
  27.9 106.4 %all-gather.5.cloned.1.call-start = ((), (), s32[]{:S(2)}) async-start(), calls=%async_computation.2 | async-start | bytes 3342336 | tf_op jit(solution)/shard_map/all_gather | solution.py:153
  28.7 227.2 %all-reduce.2.cloned.1.call-start = ((), (), s32[]{:S(2)}) async-start(), calls=%async_computation.1 | async-start | bytes 4718592 | tf_op jit(solution)/shard_map/psum | solution.py:163
  134.3 10.3 %copy-start.1 = (f32[2048,768]{1,0:T(8,128)S(1)}, f32[2048,768]{1,0:T(8,128)}, u32[]{:S(2)}) copy-start(f32[2048,768]{1,0:T(8,128)} %fusion.7) | copy-start | bytes 18874372
  163.7 94.0 %copy-start = (bf16[1,768,128]{2,1,0:T(8,128)(2,1)S(1)}, bf16[1,768,128]{2,1,0:T(8,128)(2,1)}, u32[]{:S(2)}) copy-start(bf16[1,768,128]{2,1,0:T(8,128)(2,1)} %param.9) | copy-start | bytes 589828
Sparse Core Ops, SparseCore 0:
  10.2 50.5 all-gather.6
  62.9 46.8 all-gather.4
  163.9 91.9 all-reduce.1

commit v2 on v1

--- a/solution.py
+++ b/solution.py
@@ -1,3 +1,5 @@
+import functools
+
 import jax
 import jax.numpy as jnp
 from jax import lax
@@ -6,12 +8,202 @@
 from jax.sharding import PartitionSpec as P
 
 BROWS = 128
-
-
+HI = lax.Precision.HIGHEST
 damping = 0.05
-
-
-HI = lax.Precision.HIGHEST
+MESH = pl.DeviceIdType.MESH
+PAIR = 2 * BROWS
+MESSAGES = ((0, 0), (0, 1), (1, 0), (3, 0), (1, 1), (3, 1), (2, 0), (2, 1))
+
+
+def gather_kernel(rows_avg, tok_ref, ids_ref, gate_ref, up_ref, sum_ref,
+                  tok, send, got, wg, wu, hid, acc, pack, r1, q1, r2, q2,
+                  local_sem, tok_ss, tok_rs, w_ss, w_rs, g_ss, g_rs):
+    e, d = lax.axis_index("expert"), lax.axis_index("dp")
+    y, c, x, z = e // 2, e % 2, d // 4, d % 4
+
+    def at_y(dy, dc):
+        return {"expert": ((y + dy) % 4) * 2 + (c + dc) % 2, "dp": d}
+
+    def at_x(s):
+        return {"expert": e, "dp": ((x + s) % 4) * 4 + z}
+
+    def at_z(s):
+        return {"expert": e, "dp": x * 4 + (z + s) % 4}
+
+    bar = pltpu.get_barrier_semaphore()
+    for m in MESSAGES[1:]:
+        pl.semaphore_signal(bar, inc=1, device_id=at_y(*m), device_id_type=MESH)
+    for s in (1, 2, 3):
+        pl.semaphore_signal(bar, inc=1, device_id=at_x(s), device_id_type=MESH)
+        pl.semaphore_signal(bar, inc=1, device_id=at_z(s), device_id_type=MESH)
+    load = pltpu.make_async_copy(tok_ref, tok.at[pl.ds(0, 8)], local_sem.at[0])
+    load.start()
+    own_g = pltpu.make_async_copy(gate_ref, wg.at[x, z], local_sem.at[1])
+    own_u = pltpu.make_async_copy(up_ref, wu.at[x, z], local_sem.at[2])
+    own_g.start()
+    own_u.start()
+    pl.semaphore_wait(bar, 13)
+
+    def remote(src, dst, ss, rs, to):
+        copy = pltpu.make_async_remote_copy(src_ref=src, dst_ref=dst, send_sem=ss, recv_sem=rs, device_id=to, device_id_type=MESH)
+        copy.start()
+        return copy
+
+    first = []
+    for s in (1, 2, 3):
+        first.append(remote(gate_ref, wg.at[x, z], w_ss.at[0, s - 1], w_rs.at[0, s - 1], at_x(s)))
+        first.append(remote(up_ref, wu.at[x, z], w_ss.at[1, s - 1], w_rs.at[1, s - 1], at_z(s)))
+
+    ids = [ids_ref[b] for b in range(8)]
+
+    def slots(m):
+        want = ((y + m[0]) % 4) * 2 + (c + m[1]) % 2
+        one = two = jnp.int32(8)
+        for b in range(7, -1, -1):
+            hit = ids[b] == want
+            two = jnp.where(hit, one, two)
+            one = jnp.where(hit, jnp.int32(b), one)
+        return one, two
+
+    tok[8] = jnp.zeros_like(tok[8])
+    load.wait()
+
+    def post(u):
+        for k, b in enumerate(slots(MESSAGES[u])):
+            send[u - 1, k] = tok[b]
+        return remote(send.at[u - 1], got.at[u], tok_ss.at[u - 1], tok_rs.at[u - 1], at_y(*MESSAGES[u]))
+
+    sent = {u: post(u) for u in (2, 3, 4, 5)}
+    sent[1] = post(1)
+    for k, b in enumerate(slots(MESSAGES[0])):
+        got[0, k] = tok[b]
+    acc[...] = jnp.zeros_like(acc)
+
+    own_g.wait()
+    own_u.wait()
+    for copy in first:
+        copy.wait()
+    second = []
+    for s in (1, 2, 3):
+        second.append(remote(wg.at[:, z], wg.at[:, z], w_ss.at[2, s - 1], w_rs.at[2, s - 1], at_z(s)))
+        second.append(remote(wu.at[x], wu.at[x], w_ss.at[3, s - 1], w_rs.at[3, s - 1], at_x(s)))
+
+    sent[2].wait()
+    sent[3].wait()
+    sent[6] = post(6)
+    sent[1].wait()
+    sent[4].wait()
+    sent[5].wait()
+    sent[7] = post(7)
+    for copy in second:
+        copy.wait()
+
+    model, width = 16 * wg.shape[2], wg.shape[3]
+
+    def unit(u, _):
+        @pl.when(u == 6)
+        def _():
+            sent[6].wait()
+
+        @pl.when(u == 7)
+        def _():
+            sent[7].wait()
+
+        def part(n, _):
+            cut = pl.ds(pl.multiple_of(n * 256, 256), 256)
+            rows = got[u].reshape(PAIR, model)
+            gate = jnp.dot(rows, wg[:, :, :, cut].reshape(model, 256), preferred_element_type=jnp.float32)
+            lifted = jnp.dot(rows, wu[:, :, :, cut].reshape(model, 256), preferred_element_type=jnp.float32)
+            hidden = gate / (1.0 + jnp.exp(-gate)) * lifted
+            high = hidden.astype(jnp.bfloat16)
+            low = (hidden - high.astype(jnp.float32)).astype(jnp.bfloat16)
+            hid[0:256, cut] = high
+            hid[256:512, cut] = high
+            hid[512:768, cut] = low
+            hid[768:1024, cut] = high
+            return 0
+
+        lax.fori_loop(0, width // 256, part, 0)
+        for i in range(0, width, 256):
+            acc[i:i + 256, i:] += lax.dot_general(
+                hid[0:768, i:i + 256], hid[256:1024, i:], (((0,), (0,)), ((), ())), preferred_element_type=jnp.float32
+            )
+        return 0
+
+    lax.fori_loop(0, 8, unit, 0)
+
+    for i in range(3):
+        w = width - 128 * i
+        top, low = i * 128, (5 - i) * 128
+        pack[top:top + 128, 0:w] = acc[top:top + 128, top:] * (1.0 / rows_avg)
+        pack[top:top + 128, w:] = acc[low:low + 128, low:] * (1.0 / rows_avg)
+
+    A, B = pl.ds(0, 512), pl.ds(512, 384)
+
+    def at(r, n):
+        return pl.ds(pl.multiple_of(r, 8), n)
+
+    copies = []
+    for s in (1, 2, 3):
+        tx, tz = (x + s) % 4, (z + s) % 4
+        copies.append(remote(pack.at[at(tx * 96, 96), A], r1.at[s - 1, :, A], g_ss.at[0, s - 1], g_rs.at[0, s - 1], at_x(s)))
+        copies.append(remote(pack.at[at(tz * 96, 96), B], r1.at[s - 1, :, B], g_ss.at[1, s - 1], g_rs.at[1, s - 1], at_z(s)))
+    for copy in copies:
+        copy.wait()
+    q1[:, A] = (pack[at(x * 96, 96), A] + r1[0, :, A]) + (r1[1, :, A] + r1[2, :, A])
+    q1[:, B] = (pack[at(z * 96, 96), B] + r1[0, :, B]) + (r1[1, :, B] + r1[2, :, B])
+    copies = []
+    for s in (1, 2, 3):
+        tx, tz = (x + s) % 4, (z + s) % 4
+        copies.append(remote(q1.at[at(tz * 24, 24), A], r2.at[s - 1, :, A], g_ss.at[2, s - 1], g_rs.at[2, s - 1], at_z(s)))
+        copies.append(remote(q1.at[at(tx * 24, 24), B], r2.at[s - 1, :, B], g_ss.at[3, s - 1], g_rs.at[3, s - 1], at_x(s)))
+    for copy in copies:
+        copy.wait()
+    mine_a, mine_b = at(x * 96 + z * 24, 24), at(z * 96 + x * 24, 24)
+    q2[mine_a, A] = (q1[at(z * 24, 24), A] + r2[0, :, A]) + (r2[1, :, A] + r2[2, :, A])
+    q2[mine_b, B] = (q1[at(x * 24, 24), B] + r2[0, :, B]) + (r2[1, :, B] + r2[2, :, B])
+    copies = []
+    for s in (1, 2, 3):
+        copies.append(remote(q2.at[mine_a, A], q2.at[mine_a, A], g_ss.at[4, s - 1], g_rs.at[4, s - 1], at_z(s)))
+        copies.append(remote(q2.at[mine_b, B], q2.at[mine_b, B], g_ss.at[5, s - 1], g_rs.at[5, s - 1], at_x(s)))
+    for copy in copies:
+        copy.wait()
+    row_a, row_b = at(x * 96, 96), at(z * 96, 96)
+    copies = []
+    for s in (1, 2, 3):
+        copies.append(remote(q2.at[row_a, A], q2.at[row_a, A], g_ss.at[6, s - 1], g_rs.at[6, s - 1], at_x(s)))
+        copies.append(remote(q2.at[row_b, B], q2.at[row_b, B], g_ss.at[7, s - 1], g_rs.at[7, s - 1], at_z(s)))
+    for copy in copies:
+        copy.wait()
+    sum_ref[...] = q2[...]
+
+
+def gram_sums(tokens, ids, gate, up, rows_avg):
+    model, width = tokens.shape[1], gate.shape[1]
+    any_ = pl.BlockSpec(memory_space=pl.ANY)
+    bf, f32, dma = jnp.bfloat16, jnp.float32, pltpu.SemaphoreType.DMA
+    return pl.pallas_call(
+        functools.partial(gather_kernel, float(rows_avg)),
+        out_shape=jax.ShapeDtypeStruct((width // 2, width + 128), f32),
+        in_specs=[any_, pl.BlockSpec(memory_space=pltpu.SMEM), any_, any_],
+        out_specs=pl.BlockSpec(memory_space=pltpu.VMEM),
+        scratch_shapes=[
+            pltpu.VMEM((9, BROWS, model), bf),
+            pltpu.VMEM((7, 2, BROWS, model), bf),
+            pltpu.VMEM((8, 2, BROWS, model), bf),
+            pltpu.VMEM((4, 4, model // 16, width), bf),
+            pltpu.VMEM((4, 4, model // 16, width), bf),
+            pltpu.VMEM((4 * PAIR, width), bf),
+            pltpu.VMEM((width, width), f32),
+            pltpu.VMEM((width // 2, width + 128), f32),
+            pltpu.VMEM((3, width // 8, width + 128), f32),
+            pltpu.VMEM((width // 8, width + 128), f32),
+            pltpu.VMEM((3, width // 32, width + 128), f32),
+            pltpu.VMEM((width // 2, width + 128), f32),
+            dma((3,)), dma((7,)), dma((7,)), dma((4, 3)), dma((4, 3)), dma((8, 3)), dma((8, 3)),
+        ],
+        compiler_params=pltpu.CompilerParams(collective_id=1, has_side_effects=True, vmem_limit_bytes=56 << 20),
+    )(tokens.reshape(8, BROWS, model), ids, gate, up)
 
 
 def lanes(v, k):
@@ -59,7 +251,13 @@
     return up, lo
 
 def kernel(me_ref, g_ref, w_ref, r_ref, p_ref, A, R, L):
-    A[...] = g_ref[...]
+    same = lax.broadcasted_iota(jnp.int32, (128, 128), 0) == lax.broadcasted_iota(jnp.int32, (128, 128), 1)
+    for i in range(6):
+        top, y, w = min(i, 5 - i) * 128, i * 128, 768 - 128 * i
+        lead = 0 if i < 3 else 896 - w
+        A[y:y+128, y:y+128] = g_ref[top:top+128, lead:lead+128] + jnp.where(same, damping, 0.0)
+        if w > 128:
+            A[y:y+128, y+128:] = g_ref[top:top+128, lead+128:lead+w]
     def body(kb, _):
         row = pl.multiple_of(kb*128, 128)
         blk = A[pl.ds(row,128), pl.ds(row,128)]
@@ -95,72 +293,9 @@
         compiler_params=pltpu.CompilerParams(vmem_limit_bytes=40<<20))(me, g, w)
 
 
-def fill_kernel(source_ref, block_ref, slot_ref):
-    used = source_ref[pl.program_id(0)] < source_ref[source_ref.shape[0] - 1]
-
-    @pl.when(used)
-    def _():
-        slot_ref[...] = block_ref[...]
-
-    @pl.when(jnp.logical_not(used))
-    def _():
-        slot_ref[...] = jnp.zeros_like(slot_ref)
-
-
-def fill_slots(source, blocks):
-    count, rows, model = blocks.shape
-    slots = source.shape[0]
-    return pl.pallas_call(
-        fill_kernel,
-        out_shape=jax.ShapeDtypeStruct((slots, rows, model), blocks.dtype),
-        grid_spec=pltpu.PrefetchScalarGridSpec(
-            num_scalar_prefetch=1,
-            grid=(slots,),
-            in_specs=[pl.BlockSpec((1, rows, model), lambda s, src: (lax.rem(src[s], count), 0, 0))],
-            out_specs=pl.BlockSpec((1, rows, model), lambda s, src: (s, 0, 0)),
-        ),
-    )(jnp.append(source, count), blocks)
-
-
 def on_device(tokens, block_expert, gate_weight, up_weight, down_weight):
-    n_expert = lax.axis_size("expert")
-    n_data = lax.axis_size("dp")
-    exp_local = gate_weight.shape[0]
-    width = gate_weight.shape[2]
-    model = tokens.shape[1]
-    experts = exp_local * n_expert
-    blk_count = block_expert.shape[0]
-    capacity = max(2, 2 * blk_count // experts)
-    rows_avg = blk_count * BROWS * n_data * n_expert // experts
-    blocks = tokens.reshape(blk_count, BROWS, model)
-    ids = block_expert[:, 0]
-    positions = jnp.arange(blk_count, dtype=jnp.int32)
-    same = ids[:, None] == ids[None, :]
-    earlier = positions[None, :] < positions[:, None]
-    ranks = jnp.sum((same & earlier).astype(jnp.int32), axis=1)
-    slots = jnp.arange(experts * capacity, dtype=jnp.int32)
-    match = (ids[None, :] == (slots // capacity)[:, None]) & (
-        ranks[None, :] == (slots % capacity)[:, None]
-    )
-    found = jnp.sum(match.astype(jnp.int32), axis=1)
-    source = jnp.sum(match.astype(jnp.int32) * positions[None, :], axis=1) + (1 - found) * blk_count
-    outgoing = fill_slots(source, blocks).reshape(n_expert, exp_local, capacity, BROWS, model)
-    arrived = lax.all_to_all(outgoing, "expert", split_axis=0, concat_axis=0, tiled=True)
-    eye = jnp.eye(width, dtype=jnp.float32)
-    rows = arrived[:, 0].reshape(-1, model)
-    gate = jnp.dot(
-        rows,
-        lax.all_gather(gate_weight[0], "dp", axis=0, tiled=True),
-        preferred_element_type=jnp.float32,
-    )
-    lifted = jnp.dot(
-        rows,
-        lax.all_gather(up_weight[0], "dp", axis=0, tiled=True),
-        preferred_element_type=jnp.float32,
-    )
-    hidden = jax.nn.silu(gate) * lifted
-    gram = jnp.dot(hidden.T, hidden, precision=lax.Precision.HIGHEST) / float(rows_avg)
-    total = lax.psum(gram, "dp") + damping * eye
+    rows_avg = tokens.shape[0] * lax.axis_size("expert") * lax.axis_size("dp") // lax.axis_size("expert")
+    total = gram_sums(tokens, block_expert[:, 0], gate_weight[0], up_weight[0], rows_avg)
     me = lax.axis_index("dp").astype(jnp.int32).reshape(1)
     factor, product = chol(me, total, down_weight[0])
     return (factor[None], product[None])

time: 294 us -> 180 us (0.61)
  the two profiles are of different devices: /device:TPU:0 before, /device:TPU:17 now
where the time goes in v2:
time: 180 us
  Pallas kernels  178 us (99%)
    pallas_call x1, Pallas kernels, gram_sums(): pl.pallas_call(functools.partial(gather_kernel, float(rows_avg)), out_sha...  148 us
    pallas_call x1, Pallas kernels, chol(): pl.pallas_call(kernel, out_shape=(jax.ShapeDtypeStruct((48, 768), jnp.flo...  29.7 us

profile of v2, /device:TPU:17, one launch (start us, length us, event | category | flops | bytes accessed | tf_op | source)
XLA Modules:
  0.0 180.0 jit_solution(2439873832904776212)
XLA Ops:
  0.6 0.0 copy-start.1
  0.6 148.4 %shard_map.68.g_ref = f32[384,896]{1,0:T(8,128)} custom-call(bf16[8,128,2048]{2,1,0:T(8,128)(2,1)} %bitcast.9, s32[8]{0:T(128)} %bitcast.12, bf16[128,768]{1,0:T(8,128)(2,1)} %bitcast.10, bf16[128,768]{1,0:T(8,128)(2,1)} %bitcast.11), custom_call_target="tpu_custom_call" | custom-call | tf_op jit(solution)/shard_map/pallas_call | solution.py:185
  149.0 0.0 copy-done.1
  149.0 0.0 copy-start
  149.0 1.3 copy-done
  150.4 29.7 %shard_map.69 = (f32[48,768]{1,0:T(8,128)}, f32[768,128]{1,0:T(8,128)}) custom-call(s32[1]{0:T(128)} %bitcast.me_ref, f32[384,896]{1,0:T(8,128)S(1)} %copy-done, bf16[768,128]{1,0:T(8,128)(2,1)S(1)} %bitcast.8), custom_call_target="tpu_custom_call" | custom-call | tf_op jit(solution)/shard_map/pallas_call | solution.py:290
Async XLA Ops:
  0.6 148.4 %copy-start.1 = (bf16[1,768,128]{2,1,0:T(8,128)(2,1)S(1)}, bf16[1,768,128]{2,1,0:T(8,128)(2,1)}, u32[]{:S(2)}) copy-start(bf16[1,768,128]{2,1,0:T(8,128)(2,1)} %param.9) | copy-start | bytes 589828
  149.0 1.3 copy-start

commit v3 on v2

v3 whole, which is shorter than its diff:
```python
import functools

import jax
import jax.numpy as jnp
from jax import lax
from jax.experimental import pallas as pl
from jax.experimental.pallas import tpu as pltpu
from jax.sharding import PartitionSpec as P

BROWS = 128
HI = lax.Precision.HIGHEST
damping = 0.05
MESH = pl.DeviceIdType.MESH
PAIR = 2 * BROWS
NEAR = ((0, 1, 0, 1, 0), (0, 1, 1, 1, 1))
STEPS = (
    ((2, 0, 0, 2, 0),),
    ((2, 0, 1, 2, 1),),
    ((2, 1, 0, 3, 0),),
    ((2, 1, 1, 3, 1),),
    ((1, 0, 0, 4, 0), (3, 0, 0, 4, 1)),
    ((1, 0, 1, 5, 0), (3, 0, 1, 5, 1)),
    ((1, 1, 0, 6, 0), (3, 1, 0, 6, 1)),
    ((1, 1, 1, 7, 0), (3, 1, 1, 7, 1)),
)
AHEAD = 3


def whole_kernel(rows_avg, tok_ref, ids_ref, gate_ref, up_ref, down_ref, r_ref, p_ref,
                  tok, send, got, wg, wu, hid, acc, pack, r1, q1, r2, q2, down, A, R, L,
                  local_sem, tok_ss, tok_rs, w_ss, w_rs, g_ss, g_rs):
    e, d = lax.axis_index("expert"), lax.axis_index("dp")
    y, c, x, z = e // 2, e % 2, d // 4, d % 4

    def at_y(dy, dc):
        return {"expert": ((y + dy) % 4) * 2 + (c + dc) % 2, "dp": d}

    def at_x(s):
        return {"expert": e, "dp": ((x + s) % 4) * 4 + z}

    def at_z(s):
        return {"expert": e, "dp": x * 4 + (z + s) % 4}

    bar = pltpu.get_barrier_semaphore()
    for dy, dc in ((0, 1), (1, 0), (1, 1), (2, 0), (2, 1), (3, 0), (3, 1)):
        pl.semaphore_signal(bar, inc=1, device_id=at_y(dy, dc), device_id_type=MESH)
    for s in (1, 2, 3):
        pl.semaphore_signal(bar, inc=1, device_id=at_x(s), device_id_type=MESH)
        pl.semaphore_signal(bar, inc=1, device_id=at_z(s), device_id_type=MESH)
    load = pltpu.make_async_copy(tok_ref, tok.at[pl.ds(0, 8)], local_sem.at[0])
    load.start()
    own_g = pltpu.make_async_copy(gate_ref, wg.at[x, z], local_sem.at[1])
    own_u = pltpu.make_async_copy(up_ref, wu.at[x, z], local_sem.at[2])
    own_d = pltpu.make_async_copy(down_ref, down, local_sem.at[3])
    own_d.start()
    own_g.start()
    own_u.start()
    pl.semaphore_wait(bar, 13)

    def remote(src, dst, ss, rs, to):
        copy = pltpu.make_async_remote_copy(src_ref=src, dst_ref=dst, send_sem=ss, recv_sem=rs, device_id=to, device_id_type=MESH)
        copy.start()
        return copy

    first = []
    for s in (1, 2, 3):
        first.append(remote(gate_ref, wg.at[x, z], w_ss.at[0, s - 1], w_rs.at[0, s - 1], at_x(s)))
        first.append(remote(up_ref, wu.at[x, z], w_ss.at[1, s - 1], w_rs.at[1, s - 1], at_z(s)))

    ids = [ids_ref[b] for b in range(8)]

    def slot(dy, dc, second):
        want = ((y + dy) % 4) * 2 + (c + dc) % 2
        one = two = jnp.int32(8)
        for b in range(7, -1, -1):
            hit = ids[b] == want
            two = jnp.where(hit, one, two)
            one = jnp.where(hit, jnp.int32(b), one)
        return two if second else one

    tok[8] = jnp.zeros_like(tok[8])
    load.wait()

    def block_copy(dy, dc, second, u, half):
        return pltpu.make_async_remote_copy(
            src_ref=send.at[u, half], dst_ref=got.at[u, half], send_sem=tok_ss.at[u, half], recv_sem=tok_rs.at[u, half],
            device_id=at_y(dy, dc), device_id_type=MESH,
        )

    def post(blocks):
        for b in blocks:
            send[b[3], b[4]] = tok[slot(*b[:3])]
            block_copy(*b).start()

    def sent(blocks):
        for b in blocks:
            block_copy(*b).wait_send()

    for n in range(AHEAD):
        post(STEPS[n])
    post(NEAR)
    for k in range(2):
        got[0, k] = tok[slot(0, 0, k)]
    acc[...] = jnp.zeros_like(acc)
    A[...] = jnp.zeros_like(A)
    R[...] = jnp.zeros_like(R)

    own_g.wait()
    own_u.wait()
    for copy in first:
        copy.wait()
    second = []
    for s in (1, 2, 3):
        second.append(remote(wg.at[:, z], wg.at[:, z], w_ss.at[2, s - 1], w_rs.at[2, s - 1], at_z(s)))
        second.append(remote(wu.at[x], wu.at[x], w_ss.at[3, s - 1], w_rs.at[3, s - 1], at_x(s)))
    for n in range(AHEAD, 6):
        sent(STEPS[n - AHEAD])
        post(STEPS[n])
    sent(NEAR)
    for copy in second:
        copy.wait()

    model, width = 16 * wg.shape[2], wg.shape[3]

    def unit(u, _):
        for n in (6, 7):
            @pl.when(u == n - 3)
            def _():
                sent(STEPS[n - AHEAD])
                post(STEPS[n])

        for blocks in (NEAR, STEPS[0] + STEPS[1], STEPS[2] + STEPS[3]) + STEPS[4:]:
            @pl.when(u == blocks[0][3])
            def _():
                for b in blocks:
                    block_copy(*b).wait_recv()

        def part(n, _):
            cut = pl.ds(pl.multiple_of(n * 256, 256), 256)
            rows = got[u].reshape(PAIR, model)
            gate = jnp.dot(rows, wg[:, :, :, cut].reshape(model, 256), preferred_element_type=jnp.float32)
            lifted = jnp.dot(rows, wu[:, :, :, cut].reshape(model, 256), preferred_element_type=jnp.float32)
            hidden = gate / (1.0 + jnp.exp(-gate)) * lifted
            high = hidden.astype(jnp.bfloat16)
            low = (hidden - high.astype(jnp.float32)).astype(jnp.bfloat16)
            hid[0:256, cut] = high
            hid[256:512, cut] = high
            hid[512:768, cut] = low
            hid[768:1024, cut] = high
            return 0

        lax.fori_loop(0, width // 256, part, 0)
        for i in range(0, width, 256):
            acc[i:i + 256, i:] += lax.dot_general(
                hid[0:768, i:i + 256], hid[256:1024, i:], (((0,), (0,)), ((), ())), preferred_element_type=jnp.float32
            )
        return 0

    lax.fori_loop(0, 8, unit, 0)
    for n in range(8 - AHEAD, 8):
        sent(STEPS[n])

    def fill(i):
        w = width - 128 * i
        top, low = i * 128, (5 - i) * 128
        pack[i, :, 0:w] = acc[top:top + 128, top:] * (1.0 / rows_avg)
        pack[i, :, w:] = acc[low:low + 128, low:] * (1.0 / rows_avg)

    CA, CB = pl.ds(0, 512), pl.ds(512, 384)

    def at(r, n):
        return pl.ds(pl.multiple_of(r, 8), n)

    mine_a, mine_b = at(x * 32 + z * 8, 8), at(z * 32 + x * 8, 8)

    def stage(i, k):
        out = []
        for s in (1, 2, 3):
            tx, tz = (x + s) % 4, (z + s) % 4
            if k == 0:
                a = pack.at[i, at(tx * 32, 32), CA], r1.at[i, s - 1, :, CA], at_x(s)
                b = pack.at[i, at(tz * 32, 32), CB], r1.at[i, s - 1, :, CB], at_z(s)
            elif k == 1:
                a = q1.at[i, at(tz * 8, 8), CA], r2.at[i, s - 1, :, CA], at_z(s)
                b = q1.at[i, at(tx * 8, 8), CB], r2.at[i, s - 1, :, CB], at_x(s)
            elif k == 2:
                a = q2.at[i, mine_a, CA], q2.at[i, mine_a, CA], at_z(s)
                b = q2.at[i, mine_b, CB], q2.at[i, mine_b, CB], at_x(s)
            else:
                a = q2.at[i, at(x * 32, 32), CA], q2.at[i, at(x * 32, 32), CA], at_x(s)
                b = q2.at[i, at(z * 32, 32), CB], q2.at[i, at(z * 32, 32), CB], at_z(s)
            for h, (src, dst, to) in enumerate((a, b)):
                out.append(pltpu.make_async_remote_copy(
                    src_ref=src, dst_ref=dst, send_sem=g_ss.at[i, k, h, s - 1], recv_sem=g_rs.at[i, k, h, s - 1],
                    device_id=to, device_id_type=MESH,
                ))
        return out

    def begin(i, k):
        for copy in stage(i, k):
            copy.start()

    def after(i, k):
        for copy in stage(i, k):
            copy.wait()
        if k == 0:
            q1[i, :, CA] = (pack[i, at(x * 32, 32), CA] + r1[i, 0, :, CA]) + (r1[i, 1, :, CA] + r1[i, 2, :, CA])
            q1[i, :, CB] = (pack[i, at(z * 32, 32), CB] + r1[i, 0, :, CB]) + (r1[i, 1, :, CB] + r1[i, 2, :, CB])
        elif k == 1:
            q2[i, mine_a, CA] = (q1[i, at(z * 8, 8), CA] + r2[i, 0, :, CA]) + (r2[i, 1, :, CA] + r2[i, 2, :, CA])
            q2[i, mine_b, CB] = (q1[i, at(x * 8, 8), CB] + r2[i, 0, :, CB]) + (r2[i, 1, :, CB] + r2[i, 2, :, CB])
        if k < 3:
            begin(i, k + 1)
            return
        same = lax.broadcasted_iota(jnp.int32, (128, 128), 0) == lax.broadcasted_iota(jnp.int32, (128, 128), 1)
        for b in (i, 5 - i):
            y0, w = b * 128, width - 128 * b
            lead = 0 if b < 3 else width + 128 - w
            A[y0:y0 + 128, y0:y0 + 128] += q2[i, :, lead:lead + 128] + jnp.where(same, damping, 0.0)
            if w > 128:
                A[y0:y0 + 128, y0 + 128:] += q2[i, :, lead + 128:lead + w]

    fill(0)
    begin(0, 0)
    fill(1)
    begin(1, 0)
    fill(2)
    after(0, 0)
    begin(2, 0)
    after(0, 1)
    after(1, 0)
    after(0, 2)
    after(1, 1)
    after(2, 0)
    after(1, 2)
    after(0, 3)

    def body(kb, _):
        row = pl.multiple_of(kb * 128, 128)
        for q in (1, 2):
            @pl.when(kb == q)
            def _():
                after(q, 3)

        blk = A[pl.ds(row, 128), pl.ds(row, 128)]
        up, lo = factor8([blk[8 * t:8 * t + 8] for t in range(16)])

        @pl.when(kb == 0)
        def _():
            after(2, 1)

        for t in range(16):
            R[pl.ds(row + 8 * t, 8), pl.ds(row, 128)] = up[t]
            L[8 * t:8 * t + 8, :] = lo[t]
        for q in range(5):
            @pl.when(kb == q)
            def _():
                x0 = (q + 1) * 128
                panel = jnp.dot(L[...], A[q * 128:x0, x0:], precision=HI, preferred_element_type=jnp.float32)
                R[q * 128:x0, x0:] = panel
                if q == 0:
                    after(2, 2)
                for i in range(q + 1, 6):
                    y0 = i * 128
                    A[y0:y0 + 128, y0:] -= lax.dot_general(
                        panel[:, y0 - x0:y0 - x0 + 128], panel[:, y0 - x0:], (((0,), (0,)), ((), ())), precision=HI,
                        preferred_element_type=jnp.float32,
                    )
        return 0

    lax.fori_loop(0, 6, body, 0)
    r_ref[...] = R[at(d * 48, 48), :]
    own_d.wait()
    for i in range(6):
        y0 = i * 128
        p_ref[y0:y0 + 128, :] = jnp.dot(
            R[y0:y0 + 128, y0:], down[y0:, :].astype(jnp.float32), precision=HI, preferred_element_type=jnp.float32
        )


def lanes(v, k):
    return jnp.take_along_axis(v, jnp.full((8,128), k, jnp.int32), axis=1)
def subl(v, r):
    return jnp.broadcast_to(v[r:r+1, :], (8, 128))

def factor8(M):
    M = list(M)
    lane = lax.broadcasted_iota(jnp.int32, (8,128), 1)
    sub = lax.broadcasted_iota(jnp.int32, (8,128), 0)
    up, lo = [], []
    for q in range(16):
        k0 = 8*q
        C = {t: [lanes(M[t], k0+j) for j in range(8)] for t in range(q, 16)}
        E = list(C[q])
        own = (lane >= k0) & (lane < k0+8)
        ident = (lane == sub + k0).astype(jnp.float32)
        V = M[q]
        N = jnp.where(own, ident, M[q])
        F = N
        U = V
        dinv = jnp.zeros((8,128), jnp.float32)
        for j in range(8):
            d = subl(E[j], j)
            inv = 1.0 / d
            dinv = jnp.where(sub == j, inv, dinv)
            s = E[j] * inv
            fj = jnp.where(sub == j, 1.0 - inv, s)
            ff = jnp.where(sub > j, s, 0.0)
            for i in range(j+1, 8):
                E[i] = E[i] - fj * subl(E[i], j)
            N, F, U = N - fj * subl(N, j), F - ff * subl(F, j), U - ff * subl(U, j)
        rs = jnp.sqrt(dinv)
        U, F = U*rs, F*rs
        up.append(jnp.where(lane >= sub + k0, U, 0.0))
        lo.append(jnp.where(lane <= sub + k0, F, 0.0))
        G = [subl(N, j) for j in range(8)]
        for t in range(q+1, 16):
            base = jnp.where(own, 0.0, M[t])
            c = C[t]
            a = (c[0]*G[0] + c[1]*G[1]) + (c[2]*G[2] + c[3]*G[3])
            b = (c[4]*G[4] + c[5]*G[5]) + (c[6]*G[6] + c[7]*G[7])
            M[t] = base - (a + b)
    return up, lo

def factors(tokens, ids, gate, up, down, rows_avg):
    model, width = tokens.shape[1], gate.shape[1]
    any_, vmem = pl.BlockSpec(memory_space=pl.ANY), pl.BlockSpec(memory_space=pltpu.VMEM)
    bf, f32, dma = jnp.bfloat16, jnp.float32, pltpu.SemaphoreType.DMA
    return pl.pallas_call(
        functools.partial(whole_kernel, float(rows_avg)),
        out_shape=(jax.ShapeDtypeStruct((width // 16, width), f32), jax.ShapeDtypeStruct(down.shape, f32)),
        in_specs=[any_, pl.BlockSpec(memory_space=pltpu.SMEM), any_, any_, any_],
        out_specs=(vmem, vmem),
        scratch_shapes=[
            pltpu.VMEM((9, BROWS, model), bf),
            pltpu.VMEM((8, 2, BROWS, model), bf),
            pltpu.VMEM((8, 2, BROWS, model), bf),
            pltpu.VMEM((4, 4, model // 16, width), bf),
            pltpu.VMEM((4, 4, model // 16, width), bf),
            pltpu.VMEM((4 * PAIR, width), bf),
            pltpu.VMEM((width, width), f32),
            pltpu.VMEM((3, 128, width + 128), f32),
            pltpu.VMEM((3, 3, 32, width + 128), f32),
            pltpu.VMEM((3, 32, width + 128), f32),
            pltpu.VMEM((3, 3, 8, width + 128), f32),
            pltpu.VMEM((3, 128, width + 128), f32),
            pltpu.VMEM(down.shape, bf),
            pltpu.VMEM((width, width), f32),
            pltpu.VMEM((width, width), f32),
            pltpu.VMEM((128, 128), f32),
            dma((4,)), dma((8, 2)), dma((8, 2)), dma((4, 3)), dma((4, 3)), dma((3, 4, 2, 3)), dma((3, 4, 2, 3)),
        ],
        compiler_params=pltpu.CompilerParams(collective_id=1, has_side_effects=True, vmem_limit_bytes=58 << 20),
    )(tokens.reshape(8, BROWS, model), ids, gate, up, down)


def on_device(tokens, block_expert, gate_weight, up_weight, down_weight):
    rows_avg = tokens.shape[0] * lax.axis_size("expert") * lax.axis_size("dp") // lax.axis_size("expert")
    factor, product = factors(tokens, block_expert[:, 0], gate_weight[0], up_weight[0], down_weight[0], rows_avg)
    return (factor[None], product[None])


def solution(mesh):
    placed = (
        P(("expert", "dp"), None),
        P(("expert", "dp"), None),
        P("expert", "dp", None),
        P("expert", "dp", None),
        P("expert", None, "dp"),
    )
    return jax.shard_map(
        on_device,
        mesh=mesh,
        in_specs=placed,
        out_specs=(P("expert", "dp", None), P("expert", None, "dp")),
        check_vma=False,
    )
```

time: 180 us -> 161 us (0.89)
  the two profiles are of different devices: /device:TPU:17 before, /device:TPU:0 now
where the time goes in v3:
time: 161 us
  Pallas kernels  157 us (98%)
  local copies, waits for them, and re-layouts  3.35 us (2%)
    pallas_call x1, Pallas kernels, factors(): pl.pallas_call(functools.partial(whole_kernel, float(rows_avg)), out_shap...  157 us
    unnamed x2, local copies, waits for them, and re-layouts  3.35 us

profile of v3, /device:TPU:0, one launch (start us, length us, event | category | flops | bytes accessed | tf_op | source)
XLA Modules:
  0.0 161.1 jit_solution(167119625407712268)
XLA Ops:
  0.6 157.1 %shard_map.68 = (f32[48,768]{1,0:T(8,128)}, f32[768,128]{1,0:T(8,128)}) custom-call(bf16[8,128,2048]{2,1,0:T(8,128)(2,1)} %bitcast.7, s32[8]{0:T(128)} %bitcast.13, bf16[128,768]{1,0:T(8,128)(2,1)} %bitcast.9, bf16[128,768]{1,0:T(8,128)(2,1)} %bitcast.10, bf16[768,128]{1,0:T(8,128)(2,1)} %bitcast.11), custom_call_target="tpu_custom_call" | custom-call | tf_op jit(solution)/shard_map/pallas_call | solution.py:329
  157.7 1.6 copy.9
  159.3 1.8 %copy.10 = f32[1,768,128]{2,1,0:T(8,128)} copy(f32[1,768,128]{2,1,0:T(8,128)} %bitcast.8) | data formatting | bytes 786432

commit v4 on v3

--- a/solution.py
+++ b/solution.py
@@ -243,7 +243,7 @@
                 after(q, 3)
 
         blk = A[pl.ds(row, 128), pl.ds(row, 128)]
-        up, lo = factor8([blk[8 * t:8 * t + 8] for t in range(16)])
+        up, lo = factor([blk[8 * t:8 * t + 8] for t in range(16)], 16)
 
         @pl.when(kb == 0)
         def _():
@@ -279,48 +279,71 @@
 
 
 def lanes(v, k):
-    return jnp.take_along_axis(v, jnp.full((8,128), k, jnp.int32), axis=1)
+    return jnp.take_along_axis(v, jnp.full((8, 128), k, jnp.int32), axis=1)
+
+
 def subl(v, r):
-    return jnp.broadcast_to(v[r:r+1, :], (8, 128))
-
-def factor8(M):
-    M = list(M)
-    lane = lax.broadcasted_iota(jnp.int32, (8,128), 1)
-    sub = lax.broadcasted_iota(jnp.int32, (8,128), 0)
+    return jnp.broadcast_to(v[r:r + 1, :], (8, 128))
+
+
+def factor(M, wide):
+    M, tall = list(M), wide // 8
+    lane = lax.broadcasted_iota(jnp.int32, (8, 128), 1)
+    sub = lax.broadcasted_iota(jnp.int32, (8, 128), 0)
+    zero = jnp.zeros((8, 128), jnp.float32)
     up, lo = [], []
-    for q in range(16):
-        k0 = 8*q
-        C = {t: [lanes(M[t], k0+j) for j in range(8)] for t in range(q, 16)}
-        E = list(C[q])
-        own = (lane >= k0) & (lane < k0+8)
-        ident = (lane == sub + k0).astype(jnp.float32)
-        V = M[q]
-        N = jnp.where(own, ident, M[q])
-        F = N
-        U = V
-        dinv = jnp.zeros((8,128), jnp.float32)
-        for j in range(8):
-            d = subl(E[j], j)
-            inv = 1.0 / d
-            dinv = jnp.where(sub == j, inv, dinv)
-            s = E[j] * inv
-            fj = jnp.where(sub == j, 1.0 - inv, s)
-            ff = jnp.where(sub > j, s, 0.0)
-            for i in range(j+1, 8):
-                E[i] = E[i] - fj * subl(E[i], j)
-            N, F, U = N - fj * subl(N, j), F - ff * subl(F, j), U - ff * subl(U, j)
-        rs = jnp.sqrt(dinv)
-        U, F = U*rs, F*rs
-        up.append(jnp.where(lane >= sub + k0, U, 0.0))
-        lo.append(jnp.where(lane <= sub + k0, F, 0.0))
-        G = [subl(N, j) for j in range(8)]
-        for t in range(q+1, 16):
-            base = jnp.where(own, 0.0, M[t])
-            c = C[t]
-            a = (c[0]*G[0] + c[1]*G[1]) + (c[2]*G[2] + c[3]*G[3])
-            b = (c[4]*G[4] + c[5]*G[5]) + (c[6]*G[6] + c[7]*G[7])
-            M[t] = base - (a + b)
+    for q in range(0, 16, tall):
+        k0 = 8 * q
+        C = {t: [lanes(M[t], k0 + j) for j in range(wide)] for t in range(q, 16)}
+        E = [[C[q + h][j] for h in range(tall)] for j in range(wide)]
+        own = (lane >= k0) & (lane < k0 + wide)
+        U = [M[q + h] for h in range(tall)]
+        N = [jnp.where(own, (lane == sub + (k0 + 8 * h)).astype(jnp.float32), U[h]) for h in range(tall)]
+        F = list(N)
+        scale = [zero] * tall
+        for j in range(0, wide, 2):
+            g, r = divmod(j, 8)
+            a, b, e = subl(E[j][g], r), subl(E[j + 1][g], r), subl(E[j + 1][g], r + 1)
+            inv = 1.0 / (a * e - b * b)
+            ia = 1.0 / a
+            scale[g] = jnp.where(sub == r, ia, jnp.where(sub == r + 1, a * inv, scale[g]))
+            ai, bi, ei = a * inv, b * inv, e * inv
+            f0, f1, w0, w1 = [], [], [], []
+            for h in range(tall):
+                x0 = E[j][h] * ei - E[j + 1][h] * bi
+                x1 = E[j + 1][h] * ai - E[j][h] * bi
+                w0.append(x0 if h > g else jnp.where(sub > r + 1, x0, jnp.where(sub == r + 1, b * ia, 0.0)) if h == g else None)
+                w1.append(x1 if h > g else jnp.where(sub > r + 1, x1, 0.0) if h == g else None)
+                if h == g:
+                    x0 = jnp.where(sub == r, -ei, jnp.where(sub == r + 1, bi, x0))
+                    x1 = jnp.where(sub == r, bi, jnp.where(sub == r + 1, -ai, x1))
+                f0.append(x0)
+                f1.append(x1)
+            pair = (sub == r) | (sub == r + 1)
+
+            def jordan(V):
+                p, s = subl(V[g], r), subl(V[g], r + 1)
+                return [(jnp.where(pair, 0.0, V[h]) if h == g else V[h]) - (f0[h] * p + f1[h] * s) for h in range(tall)]
+
+            def forward(V):
+                p, s = subl(V[g], r), subl(V[g], r + 1)
+                return [V[h] if h < g else V[h] - (w0[h] * p + w1[h] * s) for h in range(tall)]
+
+            for i in range(j + 2, wide):
+                E[i] = jordan(E[i])
+            N, F, U = jordan(N), forward(F), forward(U)
+        for h in range(tall):
+            root = jnp.sqrt(scale[h])
+            up.append(jnp.where(lane >= sub + (k0 + 8 * h), U[h] * root, 0.0))
+            lo.append(jnp.where(lane <= sub + (k0 + 8 * h), F[h] * root, 0.0))
+        G = [subl(N[j // 8], j % 8) for j in range(wide)]
+        for t in range(q + tall, 16):
+            terms = [C[t][j] * G[j] for j in range(wide)]
+            while len(terms) > 1:
+                terms = [terms[i] + terms[i + 1] for i in range(0, len(terms), 2)]
+            M[t] = jnp.where(own, 0.0, M[t]) - terms[0]
     return up, lo
+
 
 def factors(tokens, ids, gate, up, down, rows_avg):
     model, width = tokens.shape[1], gate.shape[1]

time: 161 us -> 156 us (0.969)
  Pallas kernels: 157 us -> 151 us
    pallas_call x1, Pallas kernels: 157 us -> 151 us  [factors(): pl.pallas_call(functools.partial(whole_kernel, float(rows_avg)), out_shap...]
where the time goes in v4:
time: 156 us; the launch traced here: 155 us
  Pallas kernels  151 us (97%)
  local copies, waits for them, and re-layouts  3.35 us (2%)
    pallas_call x1, Pallas kernels, factors(): pl.pallas_call(functools.partial(whole_kernel, float(rows_avg)), out_shap...  151 us
    unnamed x2, local copies, waits for them, and re-layouts  3.35 us

profile of v4, /device:TPU:0, one launch (start us, length us, event | category | flops | bytes accessed | tf_op | source)
XLA Modules:
  0.0 155.5 jit_solution(6012876991925265396)
XLA Ops:
  0.6 151.5 %shard_map.68 = (f32[48,768]{1,0:T(8,128)}, f32[768,128]{1,0:T(8,128)}) custom-call(bf16[8,128,2048]{2,1,0:T(8,128)(2,1)} %bitcast.7, s32[8]{0:T(128)} %bitcast.13, bf16[128,768]{1,0:T(8,128)(2,1)} %bitcast.9, bf16[128,768]{1,0:T(8,128)(2,1)} %bitcast.10, bf16[768,128]{1,0:T(8,128)(2,1)} %bitcast.11), custom_call_target="tpu_custom_call" | custom-call | tf_op jit(solution)/shard_map/pallas_call | solution.py:352
  152.1 1.6 %copy.9 = f32[1,48,768]{2,1,0:T(8,128)} copy(f32[1,48,768]{2,1,0:T(8,128)} %bitcast.12) | data formatting | bytes 294912
  153.7 1.8 %copy.10 = f32[1,768,128]{2,1,0:T(8,128)} copy(f32[1,768,128]{2,1,0:T(8,128)} %bitcast.8) | data formatting | bytes 786432

commit v5 on v4

v5 whole, which is shorter than its diff:
```python
import functools

import jax
import jax.numpy as jnp
from jax import lax
from jax.experimental import pallas as pl
from jax.experimental.pallas import tpu as pltpu
from jax.sharding import PartitionSpec as P

BROWS = 128
HI = lax.Precision.HIGHEST
damping = 0.05
MESH = pl.DeviceIdType.MESH
PAIR = 2 * BROWS
STEPS = (
    ((2, 1, 0, 2, 2),),
    ((2, 1, 1, 2, 3),),
    ((2, 0, 0, 1, 4), (3, 1, 0, 3, 4)),
    ((2, 0, 1, 1, 5), (3, 1, 1, 3, 5)),
    ((1, 1, 0, 1, 6), (3, 0, 0, 3, 6)),
    ((1, 1, 1, 1, 7), (3, 0, 1, 3, 7)),
)
AHEAD = 3


def whole_kernel(rows_avg, tok_ref, ids_ref, gate_ref, up_ref, down_ref, r_ref, p_ref,
                 tok, send, near, got, wg, wu, hid, acc, pack, r1, q1, r2, q2, bq, bs, down, A, R, L,
                 local_sem, tok_ss, near_ss, tok_rs, w_ss, w_rs, h_ss, h_rs, g_ss, g_rs):
    e, d = lax.axis_index("expert"), lax.axis_index("dp")
    y, c, x, z = e // 2, e % 2, d // 4, d % 4
    sibling = {"expert": y * 2 + 1 - c, "dp": d}

    def at_y(dy, core):
        return {"expert": ((y + dy) % 4) * 2 + core, "dp": d}

    def at_x(s):
        return {"expert": e, "dp": ((x + s) % 4) * 4 + z}

    def at_z(s):
        return {"expert": e, "dp": x * 4 + (z + s) % 4}

    bar = pltpu.get_barrier_semaphore()
    pl.semaphore_signal(bar, inc=1, device_id=sibling, device_id_type=MESH)
    for dy in (1, 2, 3):
        for core in (0, 1):
            pl.semaphore_signal(bar, inc=1, device_id=at_y(dy, core), device_id_type=MESH)
    for s in (1, 2, 3):
        pl.semaphore_signal(bar, inc=1, device_id=at_x(s), device_id_type=MESH)
        pl.semaphore_signal(bar, inc=1, device_id=at_z(s), device_id_type=MESH)
    load = pltpu.make_async_copy(tok_ref, tok.at[pl.ds(0, 8)], local_sem.at[0])
    load.start()
    own_g = pltpu.make_async_copy(gate_ref, wg.at[0, x, z], local_sem.at[1])
    own_u = pltpu.make_async_copy(up_ref, wu.at[0, x, z], local_sem.at[2])
    own_d = pltpu.make_async_copy(down_ref, down, local_sem.at[3])
    own_d.start()
    own_g.start()
    own_u.start()
    pl.semaphore_wait(bar, 13)

    def remote(src, dst, ss, rs, to):
        return pltpu.make_async_remote_copy(src_ref=src, dst_ref=dst, send_sem=ss, recv_sem=rs, device_id=to, device_id_type=MESH)

    def weights(m, k):
        out = []
        for s in (1, 2, 3):
            if k == 0:
                a, b = gate_ref if m == 0 else wg.at[m, x, z], up_ref if m == 0 else wu.at[m, x, z]
                out.append(remote(a, wg.at[m, x, z], w_ss.at[m, 0, 0, s - 1], w_rs.at[m, 0, 0, s - 1], at_x(s)))
                out.append(remote(b, wu.at[m, x, z], w_ss.at[m, 0, 1, s - 1], w_rs.at[m, 0, 1, s - 1], at_z(s)))
            elif k == 1 and s != 2:
                out.append(remote(wg.at[m, :, z], wg.at[m, :, z], w_ss.at[m, 1, 0, s - 1], w_rs.at[m, 1, 0, s - 1], at_z(s)))
                out.append(remote(wu.at[m, x], wu.at[m, x], w_ss.at[m, 1, 1, s - 1], w_rs.at[m, 1, 1, s - 1], at_x(s)))
            elif k == 2 and s != 2:
                half, fz, fx = pl.ds(s - 1, 2), (z + 4 - s) % 4, (x + 4 - s) % 4
                a, b = wg.at[m, half, fz], wu.at[m, fx, half]
                out.append(remote(a, a, w_ss.at[m, 2, 0, s - 1], w_rs.at[m, 2, 0, s - 1], at_z(s)))
                out.append(remote(b, b, w_ss.at[m, 2, 1, s - 1], w_rs.at[m, 2, 1, s - 1], at_x(s)))
        return out

    def shard():
        return [
            remote(gate_ref, wg.at[1, x, z], h_ss.at[0], h_rs.at[0], at_y(3, 0)),
            remote(up_ref, wu.at[1, x, z], h_ss.at[1], h_rs.at[1], at_y(3, 0)),
        ]

    def start(copies):
        for copy in copies:
            copy.start()

    def wait(copies):
        for copy in copies:
            copy.wait()

    start(weights(0, 0))

    @pl.when(c == 0)
    def _():
        start(shard())

    ids = [ids_ref[b] for b in range(8)]

    def slot(dy, core, second):
        want = ((y + dy) % 4) * 2 + core
        one = two = jnp.int32(8)
        for b in range(7, -1, -1):
            hit = ids[b] == want
            two = jnp.where(hit, one, two)
            one = jnp.where(hit, jnp.int32(b), one)
        return two if second else one

    tok[8] = jnp.zeros_like(tok[8])
    load.wait()

    def block_copy(n, k):
        dy, core, _, to, u = STEPS[n][k]
        return remote(send.at[n, k], got.at[u, c], tok_ss.at[n, k], tok_rs.at[u, c], at_y(to, core))

    def post(n):
        for k, b in enumerate(STEPS[n]):
            send[n, k] = tok[slot(*b[:3])]
            block_copy(n, k).start()

    def sent(n):
        for k in range(len(STEPS[n])):
            block_copy(n, k).wait_send()

    def near_copy(u, k):
        return remote(near.at[u // 2, k], got.at[u, k], near_ss.at[u // 2, k], tok_rs.at[u, k], sibling)

    for n in range(AHEAD):
        post(n)
    for k in range(2):
        near[0, k] = tok[slot(0, 1 - c, k)]
        near_copy(1, k).start()
        got[0, k] = tok[slot(0, c, k)]

    @pl.when(c == 0)
    def _():
        for k in range(2):
            got[2, k] = tok[slot(1, 0, k)]

    @pl.when(c == 1)
    def _():
        for k in range(2):
            near[1, k] = tok[slot(1, 0, k)]
            near_copy(3, k).start()

    acc[...] = jnp.zeros_like(acc)
    A[...] = jnp.zeros_like(A)
    R[...] = jnp.zeros_like(R)

    own_g.wait()
    own_u.wait()
    wait(weights(0, 0))
    start(weights(0, 1))

    @pl.when(c == 0)
    def _():
        wait(shard())
        start(weights(1, 0))

    wait(weights(0, 1))
    start(weights(0, 2))

    @pl.when(c == 0)
    def _():
        wait(weights(1, 0))
        start(weights(1, 1))

    for n in range(AHEAD, len(STEPS)):
        sent(n - AHEAD)
        post(n)
    for k in range(2):
        near_copy(1, k).wait_send()

    @pl.when(c == 1)
    def _():
        for k in range(2):
            near_copy(3, k).wait_send()

    wait(weights(0, 2))
    model, width = 16 * wg.shape[3], wg.shape[4]

    def landed(u):
        for k in range(2):
            remote(near.at[0, k], got.at[u, k], near_ss.at[0, k], tok_rs.at[u, k], sibling).wait_recv()

    CA, CB = pl.ds(0, 512), pl.ds(512, 384)

    def at(r, n):
        return pl.ds(pl.multiple_of(r, 8), n)

    mine_a, mine_b = at(x * 32 + z * 8, 8), at(z * 32 + x * 8, 8)

    def fill(m, i):
        w = width - 128 * i
        top, low = i * 128, (5 - i) * 128
        pack[m, i, :, 0:w] = acc[m, top:top + 128, top:] * (1.0 / rows_avg)
        pack[m, i, :, w:] = acc[m, low:low + 128, low:] * (1.0 / rows_avg)

    def stage(m, i, k):
        out = []
        for s in (1, 2, 3):
            tx, tz = (x + s) % 4, (z + s) % 4
            if k == 0:
                a = pack.at[m, i, at(tx * 32, 32), CA], r1.at[m, i, s - 1, :, CA], at_x(s)
                b = pack.at[m, i, at(tz * 32, 32), CB], r1.at[m, i, s - 1, :, CB], at_z(s)
            elif k == 1:
                a = q1.at[m, i, at(tz * 8, 8), CA], r2.at[m, i, s - 1, :, CA], at_z(s)
                b = q1.at[m, i, at(tx * 8, 8), CB], r2.at[m, i, s - 1, :, CB], at_x(s)
            elif k == 2:
                a = q2.at[i, mine_a, CA], q2.at[i, mine_a, CA], at_z(s)
                b = q2.at[i, mine_b, CB], q2.at[i, mine_b, CB], at_x(s)
            else:
                a = q2.at[i, at(x * 32, 32), CA], q2.at[i, at(x * 32, 32), CA], at_x(s)
                b = q2.at[i, at(z * 32, 32), CB], q2.at[i, at(z * 32, 32), CB], at_z(s)
            for h, (src, dst, to) in enumerate((a, b)):
                out.append(remote(src, dst, g_ss.at[m, i, k, h, s - 1], g_rs.at[m, i, k, h, s - 1], to))
        return out

    def hop():
        return remote(bq, bs, h_ss.at[2], h_rs.at[2], at_y(1, 0))

    def begin(m, i, k):
        start(stage(m, i, k))

    def after(m, i, k):
        wait(stage(m, i, k))
        if k == 0:
            q1[m, i, :, CA] = (pack[m, i, at(x * 32, 32), CA] + r1[m, i, 0, :, CA]) + (r1[m, i, 1, :, CA] + r1[m, i, 2, :, CA])
            q1[m, i, :, CB] = (pack[m, i, at(z * 32, 32), CB] + r1[m, i, 0, :, CB]) + (r1[m, i, 1, :, CB] + r1[m, i, 2, :, CB])
        elif k == 1:
            a = (q1[m, i, at(z * 8, 8), CA] + r2[m, i, 0, :, CA]) + (r2[m, i, 1, :, CA] + r2[m, i, 2, :, CA])
            b = (q1[m, i, at(x * 8, 8), CB] + r2[m, i, 0, :, CB]) + (r2[m, i, 1, :, CB] + r2[m, i, 2, :, CB])
            if m == 1:
                bq[i, :, CA] = a
                bq[i, :, CB] = b
                return
            q2[i, mine_a, CA] = a
            q2[i, mine_b, CB] = b

            @pl.when(c == 0)
            def _():
                q2[i, mine_a, CA] += bs[i, :, CA]
                q2[i, mine_b, CB] += bs[i, :, CB]
        if k < 3:
            begin(m, i, k + 1)
            return
        same = lax.broadcasted_iota(jnp.int32, (128, 128), 0) == lax.broadcasted_iota(jnp.int32, (128, 128), 1)
        for b in (i, 5 - i):
            y0, w = b * 128, width - 128 * b
            lead = 0 if b < 3 else width + 128 - w
            A[y0:y0 + 128, y0:y0 + 128] += q2[i, :, lead:lead + 128] + jnp.where(same, damping, 0.0)
            if w > 128:
                A[y0:y0 + 128, y0 + 128:] += q2[i, :, lead + 128:lead + w]

    def unit(u, _):
        which = (1 - c) * (((u + 2) // 4) % 2)

        @pl.when((c == 0) & (u == 1))
        def _():
            wait(weights(1, 1))
            start(weights(1, 2))

        @pl.when((c == 0) & (u == 2))
        def _():
            wait(weights(1, 2))

        @pl.when((c == 0) & (u == 6))
        def _():
            for i in range(3):
                fill(1, i)
                begin(1, i, 0)

        @pl.when((c == 0) & (u == 7))
        def _():
            for i in range(3):
                after(1, i, 0)

        @pl.when((c == 1) & (u == 2))
        def _():
            landed(2)

        for n in (1, 3, 4, 5, 6, 7):
            @pl.when(u == n)
            def _():
                landed(n)

        def part(n, _):
            cut = pl.ds(pl.multiple_of(n * 256, 256), 256)
            rows = got[u].reshape(PAIR, model)
            gate = jnp.dot(rows, wg[which, :, :, :, cut].reshape(model, 256), preferred_element_type=jnp.float32)
            lifted = jnp.dot(rows, wu[which, :, :, :, cut].reshape(model, 256), preferred_element_type=jnp.float32)
            hidden = gate / (1.0 + jnp.exp(-gate)) * lifted
            high = hidden.astype(jnp.bfloat16)
            low = (hidden - high.astype(jnp.float32)).astype(jnp.bfloat16)
            hid[0:256, cut] = high
            hid[256:512, cut] = high
            hid[512:768, cut] = low
            hid[768:1024, cut] = high
            return 0

        lax.fori_loop(0, width // 256, part, 0)
        for i in range(0, width, 256):
            acc[which, i:i + 256, i:] += lax.dot_general(
                hid[0:768, i:i + 256], hid[256:1024, i:], (((0,), (0,)), ((), ())), preferred_element_type=jnp.float32
            )
        return 0

    lax.fori_loop(0, 8, unit, 0)
    fill(0, 0)
    begin(0, 0, 0)
    fill(0, 1)
    begin(0, 1, 0)

    @pl.when(c == 0)
    def _():
        for i in range(3):
            after(1, i, 1)
        hop().start()

    fill(0, 2)
    for n in range(len(STEPS) - AHEAD, len(STEPS)):
        sent(n)
    after(0, 0, 0)
    begin(0, 2, 0)

    @pl.when(c == 0)
    def _():
        hop().wait()

    after(0, 0, 1)
    after(0, 1, 0)
    after(0, 0, 2)
    after(0, 1, 1)
    after(0, 2, 0)
    after(0, 1, 2)
    after(0, 0, 3)

    def body(kb, _):
        row = pl.multiple_of(kb * 128, 128)
        for q in (1, 2):
            @pl.when(kb == q)
            def _():
                after(0, q, 3)

        blk = A[pl.ds(row, 128), pl.ds(row, 128)]
        up, lo = factor([blk[8 * t:8 * t + 8] for t in range(16)], 16)

        @pl.when(kb == 0)
        def _():
            after(0, 2, 1)

        for t in range(16):
            R[pl.ds(row + 8 * t, 8), pl.ds(row, 128)] = up[t]
            L[8 * t:8 * t + 8, :] = lo[t]
        for q in range(5):
            @pl.when(kb == q)
            def _():
                x0 = (q + 1) * 128
                panel = jnp.dot(L[...], A[q * 128:x0, x0:], precision=HI, preferred_element_type=jnp.float32)
                R[q * 128:x0, x0:] = panel
                if q == 0:
                    after(0, 2, 2)
                for i in range(q + 1, 6):
                    y0 = i * 128
                    A[y0:y0 + 128, y0:] -= lax.dot_general(
                        panel[:, y0 - x0:y0 - x0 + 128], panel[:, y0 - x0:], (((0,), (0,)), ((), ())), precision=HI,
                        preferred_element_type=jnp.float32,
                    )
        return 0

    lax.fori_loop(0, 6, body, 0)
    r_ref[...] = R[at(d * 48, 48), :]
    own_d.wait()
    for i in range(6):
        y0 = i * 128
        p_ref[y0:y0 + 128, :] = jnp.dot(
            R[y0:y0 + 128, y0:], down[y0:, :].astype(jnp.float32), precision=HI, preferred_element_type=jnp.float32
        )


def lanes(v, k):
    return jnp.take_along_axis(v, jnp.full((8, 128), k, jnp.int32), axis=1)


def subl(v, r):
    return jnp.broadcast_to(v[r:r + 1, :], (8, 128))


def factor(M, wide):
    M, tall = list(M), wide // 8
    lane = lax.broadcasted_iota(jnp.int32, (8, 128), 1)
    sub = lax.broadcasted_iota(jnp.int32, (8, 128), 0)
    zero = jnp.zeros((8, 128), jnp.float32)
    up, lo = [], []
    for q in range(0, 16, tall):
        k0 = 8 * q
        C = {t: [lanes(M[t], k0 + j) for j in range(wide)] for t in range(q, 16)}
        E = [[C[q + h][j] for h in range(tall)] for j in range(wide)]
        own = (lane >= k0) & (lane < k0 + wide)
        U = [M[q + h] for h in range(tall)]
        N = [jnp.where(own, (lane == sub + (k0 + 8 * h)).astype(jnp.float32), U[h]) for h in range(tall)]
        F = list(N)
        scale = [zero] * tall
        for j in range(0, wide, 2):
            g, r = divmod(j, 8)
            a, b, e = subl(E[j][g], r), subl(E[j + 1][g], r), subl(E[j + 1][g], r + 1)
            inv = 1.0 / (a * e - b * b)
            ia = 1.0 / a
            scale[g] = jnp.where(sub == r, ia, jnp.where(sub == r + 1, a * inv, scale[g]))
            ai, bi, ei = a * inv, b * inv, e * inv
            f0, f1, w0, w1 = [], [], [], []
            for h in range(tall):
                x0 = E[j][h] * ei - E[j + 1][h] * bi
                x1 = E[j + 1][h] * ai - E[j][h] * bi
                w0.append(x0 if h > g else jnp.where(sub > r + 1, x0, jnp.where(sub == r + 1, b * ia, 0.0)) if h == g else None)
                w1.append(x1 if h > g else jnp.where(sub > r + 1, x1, 0.0) if h == g else None)
                if h == g:
                    x0 = jnp.where(sub == r, -ei, jnp.where(sub == r + 1, bi, x0))
                    x1 = jnp.where(sub == r, bi, jnp.where(sub == r + 1, -ai, x1))
                f0.append(x0)
                f1.append(x1)
            pair = (sub == r) | (sub == r + 1)

            def jordan(V):
                p, s = subl(V[g], r), subl(V[g], r + 1)
                return [(jnp.where(pair, 0.0, V[h]) if h == g else V[h]) - (f0[h] * p + f1[h] * s) for h in range(tall)]

            def forward(V):
                p, s = subl(V[g], r), subl(V[g], r + 1)
                return [V[h] if h < g else V[h] - (w0[h] * p + w1[h] * s) for h in range(tall)]

            for i in range(j + 2, wide):
                E[i] = jordan(E[i])
            N, F, U = jordan(N), forward(F), forward(U)
        for h in range(tall):
            root = jnp.sqrt(scale[h])
            up.append(jnp.where(lane >= sub + (k0 + 8 * h), U[h] * root, 0.0))
            lo.append(jnp.where(lane <= sub + (k0 + 8 * h), F[h] * root, 0.0))
        G = [subl(N[j // 8], j % 8) for j in range(wide)]
        for t in range(q + tall, 16):
            terms = [C[t][j] * G[j] for j in range(wide)]
            while len(terms) > 1:
                terms = [terms[i] + terms[i + 1] for i in range(0, len(terms), 2)]
            M[t] = jnp.where(own, 0.0, M[t]) - terms[0]
    return up, lo


def factors(tokens, ids, gate, up, down, rows_avg):
    model, width = tokens.shape[1], gate.shape[1]
    any_, vmem = pl.BlockSpec(memory_space=pl.ANY), pl.BlockSpec(memory_space=pltpu.VMEM)
    bf, f32, dma = jnp.bfloat16, jnp.float32, pltpu.SemaphoreType.DMA
    return pl.pallas_call(
        functools.partial(whole_kernel, float(rows_avg)),
        out_shape=(jax.ShapeDtypeStruct((width // 16, width), f32), jax.ShapeDtypeStruct(down.shape, f32)),
        in_specs=[any_, pl.BlockSpec(memory_space=pltpu.SMEM), any_, any_, any_],
        out_specs=(vmem, vmem),
        scratch_shapes=[
            pltpu.VMEM((9, BROWS, model), bf),
            pltpu.VMEM((6, 2, BROWS, model), bf),
            pltpu.VMEM((2, 2, BROWS, model), bf),
            pltpu.VMEM((8, 2, BROWS, model), bf),
            pltpu.VMEM((2, 4, 4, model // 16, width), bf),
            pltpu.VMEM((2, 4, 4, model // 16, width), bf),
            pltpu.VMEM((4 * PAIR, width), bf),
            pltpu.VMEM((2, width, width), f32),
            pltpu.VMEM((2, 3, 128, width + 128), f32),
            pltpu.VMEM((2, 3, 3, 32, width + 128), f32),
            pltpu.VMEM((2, 3, 32, width + 128), f32),
            pltpu.VMEM((2, 3, 3, 8, width + 128), f32),
            pltpu.VMEM((3, 128, width + 128), f32),
            pltpu.VMEM((3, 8, width + 128), f32),
            pltpu.VMEM((3, 8, width + 128), f32),
            pltpu.VMEM(down.shape, bf),
            pltpu.VMEM((width, width), f32),
            pltpu.VMEM((width, width), f32),
            pltpu.VMEM((128, 128), f32),
            dma((4,)), dma((6, 2)), dma((2, 2)), dma((8, 2)), dma((2, 3, 2, 3)), dma((2, 3, 2, 3)), dma((3,)), dma((3,)),
            dma((2, 3, 4, 2, 3)), dma((2, 3, 4, 2, 3)),
        ],
        compiler_params=pltpu.CompilerParams(collective_id=1, has_side_effects=True, vmem_limit_bytes=60 << 20),
    )(tokens.reshape(8, BROWS, model), ids, gate, up, down)


def on_device(tokens, block_expert, gate_weight, up_weight, down_weight):
    rows_avg = tokens.shape[0] * lax.axis_size("expert") * lax.axis_size("dp") // lax.axis_size("expert")
    factor, product = factors(tokens, block_expert[:, 0], gate_weight[0], up_weight[0], down_weight[0], rows_avg)
    return (factor[None], product[None])


def solution(mesh):
    placed = (
        P(("expert", "dp"), None),
        P(("expert", "dp"), None),
        P("expert", "dp", None),
        P("expert", "dp", None),
        P("expert", None, "dp"),
    )
    return jax.shard_map(
        on_device,
        mesh=mesh,
        in_specs=placed,
        out_specs=(P("expert", "dp", None), P("expert", None, "dp")),
        check_vma=False,
    )
```

time: 156 us -> 148 us (0.949)
  Pallas kernels: 151 us -> 144 us
    pallas_call x1, Pallas kernels: 151 us -> 144 us  [factors(): pl.pallas_call(functools.partial(whole_kernel, float(rows_avg)), out_shap...]
where the time goes in v5:
time: 148 us
  Pallas kernels  144 us (97%)
  local copies, waits for them, and re-layouts  3.35 us (2%)
    pallas_call x1, Pallas kernels, factors(): pl.pallas_call(functools.partial(whole_kernel, float(rows_avg)), out_shap...  144 us
    unnamed x2, local copies, waits for them, and re-layouts  3.35 us

profile of v5, /device:TPU:0, one launch (start us, length us, event | category | flops | bytes accessed | tf_op | source)
XLA Modules:
  0.0 148.0 jit_solution(16724004112176636656)
XLA Ops:
  0.6 144.0 %shard_map.68 = (f32[48,768]{1,0:T(8,128)}, f32[768,128]{1,0:T(8,128)}) custom-call(bf16[8,128,2048]{2,1,0:T(8,128)(2,1)} %bitcast.7, s32[8]{0:T(128)} %bitcast.13, bf16[128,768]{1,0:T(8,128)(2,1)} %bitcast.9, bf16[128,768]{1,0:T(8,128)(2,1)} %bitcast.10, bf16[768,128]{1,0:T(8,128)(2,1)} %bitcast.11), custom_call_target="tpu_custom_call" | custom-call | tf_op jit(solution)/shard_map/pallas_call | solution.py:454
  144.7 1.6 %copy.9 = f32[1,48,768]{2,1,0:T(8,128)} copy(f32[1,48,768]{2,1,0:T(8,128)} %bitcast.12) | data formatting | bytes 294912
  146.3 1.8 %copy.10 = f32[1,768,128]{2,1,0:T(8,128)} copy(f32[1,768,128]{2,1,0:T(8,128)} %bitcast.8) | data formatting | bytes 786432

commit v6 on v5

--- a/solution.py
+++ b/solution.py
@@ -159,13 +159,13 @@
         wait(shard())
         start(weights(1, 0))
 
+    @pl.when(c == 0)
+    def _():
+        wait(weights(1, 0))
+        start(weights(1, 1))
+
     wait(weights(0, 1))
     start(weights(0, 2))
-
-    @pl.when(c == 0)
-    def _():
-        wait(weights(1, 0))
-        start(weights(1, 1))
 
     for n in range(AHEAD, len(STEPS)):
         sent(n - AHEAD)
@@ -177,6 +177,11 @@
     def _():
         for k in range(2):
             near_copy(3, k).wait_send()
+
+    @pl.when(c == 0)
+    def _():
+        wait(weights(1, 1))
+        start(weights(1, 2))
 
     wait(weights(0, 2))
     model, width = 16 * wg.shape[3], wg.shape[4]
@@ -257,11 +262,6 @@
     def unit(u, _):
         which = (1 - c) * (((u + 2) // 4) % 2)
 
-        @pl.when((c == 0) & (u == 1))
-        def _():
-            wait(weights(1, 1))
-            start(weights(1, 2))
-
         @pl.when((c == 0) & (u == 2))
         def _():
             wait(weights(1, 2))
@@ -271,11 +271,6 @@
             for i in range(3):
                 fill(1, i)
                 begin(1, i, 0)
-
-        @pl.when((c == 0) & (u == 7))
-        def _():
-            for i in range(3):
-                after(1, i, 0)
 
         @pl.when((c == 1) & (u == 2))
         def _():
@@ -301,6 +296,12 @@
             return 0
 
         lax.fori_loop(0, width // 256, part, 0)
+
+        @pl.when((c == 0) & (u == 7))
+        def _():
+            for i in range(3):
+                after(1, i, 0)
+
         for i in range(0, width, 256):
             acc[which, i:i + 256, i:] += lax.dot_general(
                 hid[0:768, i:i + 256], hid[256:1024, i:], (((0,), (0,)), ((), ())), preferred_element_type=jnp.float32
@@ -453,7 +454,7 @@
     bf, f32, dma = jnp.bfloat16, jnp.float32, pltpu.SemaphoreType.DMA
     return pl.pallas_call(
         functools.partial(whole_kernel, float(rows_avg)),
-        out_shape=(jax.ShapeDtypeStruct((width // 16, width), f32), jax.ShapeDtypeStruct(down.shape, f32)),
+        out_shape=(pltpu.VMEM((width // 16, width), f32), pltpu.VMEM(down.shape, f32)),
         in_specs=[any_, pl.BlockSpec(memory_space=pltpu.SMEM), any_, any_, any_],
         out_specs=(vmem, vmem),
         scratch_shapes=[

time: 148 us -> 143 us (0.966)
  Pallas kernels: 144 us -> 141 us
  local copies, waits for them, and re-layouts: 3.35 us -> 1.41 us
    pallas_call x1, Pallas kernels: 144 us -> 141 us  [factors(): pl.pallas_call(functools.partial(whole_kernel, float(rows_avg)), out_shap...]
    unnamed x2, local copies, waits for them, and re-layouts: 3.35 us -> 1.41 us
where the time goes in v6:
time: 143 us
  Pallas kernels  141 us (99%)
    pallas_call x1, Pallas kernels, factors(): pl.pallas_call(functools.partial(whole_kernel, float(rows_avg)), out_shap...  141 us

profile of v6, /device:TPU:0, one launch (start us, length us, event | category | flops | bytes accessed | tf_op | source)
XLA Modules:
  0.0 143.0 jit_solution(6552615798924983419)
XLA Ops:
  0.6 140.9 %shard_map.68 = (f32[48,768]{1,0:T(8,128)S(1)}, f32[768,128]{1,0:T(8,128)S(1)}) custom-call(bf16[8,128,2048]{2,1,0:T(8,128)(2,1)} %bitcast.9, s32[8]{0:T(128)} %bitcast.13, bf16[128,768]{1,0:T(8,128)(2,1)} %bitcast.10, bf16[128,768]{1,0:T(8,128)(2,1)} %bitcast.11, bf16[768,128]{1,0:T(8,128)(2,1)} %bitcast.12), custom_call_target="tpu_custom_call" | custom-call | tf_op jit(solution)/shard_map/pallas_call | solution.py:455
  141.6 0.7 copy.9
  142.2 0.7 copy.10

commit v7 on v6

--- a/solution.py
+++ b/solution.py
@@ -336,7 +336,16 @@
     after(0, 1, 1)
     after(0, 2, 0)
     after(0, 1, 2)
+    after(0, 2, 1)
     after(0, 0, 3)
+
+    own_d.wait()
+
+    def product(i):
+        y0 = i * 128
+        p_ref[y0:y0 + 128, :] = jnp.dot(
+            R[y0:y0 + 128, y0:], down[y0:, :].astype(jnp.float32), precision=HI, preferred_element_type=jnp.float32
+        )
 
     def body(kb, _):
         row = pl.multiple_of(kb * 128, 128)
@@ -350,7 +359,7 @@
 
         @pl.when(kb == 0)
         def _():
-            after(0, 2, 1)
+            after(0, 2, 2)
 
         for t in range(16):
             R[pl.ds(row + 8 * t, 8), pl.ds(row, 128)] = up[t]
@@ -361,8 +370,7 @@
                 x0 = (q + 1) * 128
                 panel = jnp.dot(L[...], A[q * 128:x0, x0:], precision=HI, preferred_element_type=jnp.float32)
                 R[q * 128:x0, x0:] = panel
-                if q == 0:
-                    after(0, 2, 2)
+                product(q)
                 for i in range(q + 1, 6):
                     y0 = i * 128
                     A[y0:y0 + 128, y0:] -= lax.dot_general(
@@ -372,13 +380,8 @@
         return 0
 
     lax.fori_loop(0, 6, body, 0)
+    product(5)
     r_ref[...] = R[at(d * 48, 48), :]
-    own_d.wait()
-    for i in range(6):
-        y0 = i * 128
-        p_ref[y0:y0 + 128, :] = jnp.dot(
-            R[y0:y0 + 128, y0:], down[y0:, :].astype(jnp.float32), precision=HI, preferred_element_type=jnp.float32
-        )
 
 
 def lanes(v, k):

time: 143 us -> 142 us (level)
  no operation moved by 1% of the time
where the time goes in v7:
time: 142 us
  Pallas kernels  140 us (99%)
    pallas_call x1, Pallas kernels, factors(): pl.pallas_call(functools.partial(whole_kernel, float(rows_avg)), out_shap...  140 us

profile of v7, /device:TPU:0, one launch (start us, length us, event | category | flops | bytes accessed | tf_op | source)
XLA Modules:
  0.0 141.6 jit_solution(9042588252176940877)
XLA Ops:
  0.6 139.5 %shard_map.68 = (f32[48,768]{1,0:T(8,128)S(1)}, f32[768,128]{1,0:T(8,128)S(1)}) custom-call(bf16[8,128,2048]{2,1,0:T(8,128)(2,1)} %bitcast.9, s32[8]{0:T(128)} %bitcast.13, bf16[128,768]{1,0:T(8,128)(2,1)} %bitcast.10, bf16[128,768]{1,0:T(8,128)(2,1)} %bitcast.11, bf16[768,128]{1,0:T(8,128)(2,1)} %bitcast.12), custom_call_target="tpu_custom_call" | custom-call | tf_op jit(solution)/shard_map/pallas_call | solution.py:458
  140.2 0.7 copy.9
  140.8 0.7 copy.10

commit v8 on v7

--- a/solution.py
+++ b/solution.py
@@ -20,7 +20,7 @@
     ((1, 1, 0, 1, 6), (3, 0, 0, 3, 6)),
     ((1, 1, 1, 1, 7), (3, 0, 1, 3, 7)),
 )
-AHEAD = 3
+AHEAD = 4
 
 
 def whole_kernel(rows_avg, tok_ref, ids_ref, gate_ref, up_ref, down_ref, r_ref, p_ref,

time: 142 us -> 142 us (level)
  no operation moved by 1% of the time
where the time goes in v8:
time: 142 us
  Pallas kernels  140 us (99%)
    pallas_call x1, Pallas kernels, factors(): pl.pallas_call(functools.partial(whole_kernel, float(rows_avg)), out_shap...  140 us

profile of v8, /device:TPU:0, one launch (start us, length us, event | category | flops | bytes accessed | tf_op | source)
XLA Modules:
  0.0 141.6 jit_solution(13195999027244735837)
XLA Ops:
  0.6 139.5 %shard_map.68 = (f32[48,768]{1,0:T(8,128)S(1)}, f32[768,128]{1,0:T(8,128)S(1)}) custom-call(bf16[8,128,2048]{2,1,0:T(8,128)(2,1)} %bitcast.9, s32[8]{0:T(128)} %bitcast.13, bf16[128,768]{1,0:T(8,128)(2,1)} %bitcast.10, bf16[128,768]{1,0:T(8,128)(2,1)} %bitcast.11, bf16[768,128]{1,0:T(8,128)(2,1)} %bitcast.12), custom_call_target="tpu_custom_call" | custom-call | tf_op jit(solution)/shard_map/pallas_call | solution.py:458
  140.2 0.7 copy.9
  140.8 0.7 copy.10
